TPU v7x, 256 devices: a whole 4x4x8 slice. The times are simulated.
256 devices in a mesh: rows: 128 (over x, y, z), cols: 2 (over core).
Axes of the slice: x: 4, y: 4, z: 8, core: 2. Of those that a mesh axis runs over, the one named last changes fastest.
Arguments:
- whitening: float32 [49152, 384], P('rows'), as said below
- sensor_states: int32 [49152, 4], P('rows'), may hold values from 0 to 1023, as said below
- sensor_coefficients: float32 [49152, 4], P('rows'), may hold values from -5 to 5
- sensor_readings: float32 [49152], P('rows'), may hold values from -6 to 6
- conduit_endpoints: int32 [16384, 2], P('rows'), may hold values from 0 to 1023
- conductance: float32 [16384], P('rows'), may hold values from 0.2 to 1
- balance_right_side: float32 [16384], P('rows'), may hold values from -3 to 3
- prior_root_factor: float32 [1024, 1024], P('rows'), as said below
- prior_information: float32 [1024], P('rows'), may hold values from -6 to 6
- transition: float32 [1024, 1024], P('cols'), may hold values from -0.1875 to 0.1875
Outputs:
- r_post: float32 [1024, 1024], P('rows', 'cols')
- z_post: float32 [1024], P('cols')
- x_next: float32 [1024], P('cols')
Inputs may be any that keep to these rules, and one draw needn't show every extreme that they name: `prior_root_factor`: upper triangular, with diagonal entries between 1.5 and 3. `whitening`: each aligned block of 384 rows is a lower triangular matrix with a positive diagonal. `sensor_states`: the 4 states of a row are consecutive, counted modulo 1024.
All inputs are finite; a program needn't handle non-finite values.
Results may differ from a plain program's by a relative error of at most 0.0003.
Values sent between devices are 32-bit elements; how exact they have to be, the bound alone decides.
A program may use at most 128 MiB of HBM per device.

v0:
```python
import jax
import jax.numpy as jnp
from jax import lax
from jax.sharding import PartitionSpec as P


def incidence_matrix(states, coeffs, state_total_count):
    column_ids = lax.broadcasted_iota(jnp.int32, (states.shape[0], state_total_count), 1)
    summed = jnp.zeros((states.shape[0], state_total_count), jnp.float32)
    for position in range(states.shape[1]):
        summed = summed + jnp.where(
            column_ids == states[:, position : position + 1],
            coeffs[:, position : position + 1],
            0.0,
        )
    return summed


def per_device(
    whitening,
    sensor_states,
    sensor_coefficients,
    sensor_readings,
    conduit_endpoints,
    conductance,
    balance_right_side,
    prior_root_factor,
    prior_information,
    transition,
):
    highest_accuracy = lax.Precision.HIGHEST
    state_total_count = prior_root_factor.shape[1]
    col_width = state_total_count // lax.axis_size("cols")
    col_start = lax.axis_index("cols") * col_width
    sensed_states = incidence_matrix(sensor_states, sensor_coefficients, state_total_count)
    sensor_row_list = jnp.dot(whitening, sensed_states, precision=highest_accuracy)
    sensor_right_side = jnp.dot(whitening, sensor_readings, precision=highest_accuracy)
    pair_coeffs = jnp.stack([conductance, -conductance], axis=1)
    balance_row_list = incidence_matrix(conduit_endpoints, pair_coeffs, state_total_count)
    stacked_system = jnp.concatenate([prior_root_factor, sensor_row_list, balance_row_list], axis=0)
    combined_right_side = jnp.concatenate(
        [prior_information, sensor_right_side, conductance * balance_right_side], axis=0
    )
    moment_part = lax.dot_general(
        stacked_system, combined_right_side, (((0,), (0,)), ((), ())), precision=highest_accuracy
    )
    stacked_cols = lax.dynamic_slice_in_dim(stacked_system, col_start, col_width, 1)
    gram_part = lax.dot_general(
        stacked_system, stacked_cols, (((0,), (0,)), ((), ())), precision=highest_accuracy
    )
    gram_sum, moment = lax.psum((gram_part, moment_part), "rows")
    gram = lax.all_gather(gram_sum, "cols", axis=1, tiled=True)
    lower_factor = jnp.linalg.cholesky(gram)
    z_col = lax.linalg.triangular_solve(lower_factor, moment[:, None], left_side=True, lower=True)
    est_col = lax.linalg.triangular_solve(
        lower_factor, z_col, left_side=True, lower=True, transpose_a=True
    )
    row_count = state_total_count // lax.axis_size("rows")
    row_start = lax.axis_index("rows") * row_count
    factor_piece = lax.dynamic_slice(lower_factor, (col_start, row_start), (col_width, row_count)).T
    z_piece = lax.dynamic_slice_in_dim(z_col[:, 0], col_start, col_width, 0)
    x_piece = jnp.dot(transition, est_col[:, 0], precision=highest_accuracy)
    return (factor_piece, z_piece, x_piece)


def solution(mesh):
    in_specs = (
        P("rows", None),
        P("rows", None),
        P("rows", None),
        P("rows"),
        P("rows", None),
        P("rows"),
        P("rows"),
        P("rows", None),
        P("rows"),
        P("cols", None),
    )
    out_specs = (P("rows", "cols"), P("cols"), P("cols"))
    return jax.shard_map(
        per_device, mesh=mesh, in_specs=in_specs, out_specs=out_specs, check_vma=False
    )
```

profile of v0, /device:TPU:0, one launch (start us, length us, event | category | flops | bytes accessed | tf_op | source)
XLA Modules:
  0.0 962.5 jit_solution(1284550120167639939)
XLA Ops:
  11.3 4.6 fusion.10
  17.3 6.6 fusion.42
  24.0 227.8 %all-reduce.3.cloned.1.call-done = f32[1024,512]{0,1:T(8,128)} async-done(((f32[1024,512]{0,1:T(8,128)}), f32[1024,512]{0,1:T(8,128)}) %all-reduce.3.cloned.1.call-update) | async-done | bytes 2097168 | tf_op jit(solution)/shard_map/psum | solution.py:51
  252.6 2.6 fusion.142
  255.2 347.1 %psum.15 = f32[1024]{0:T(1024)S(1)} all-reduce(f32[1024]{0:T(1024)S(1)} %bitcast.355), channel_id=1, replica_groups=mesh['rows'=128,'cols'=2] {'rows'}, use_global_device_ids=true, to_apply=%region_17.18 | all-reduce | flops 1024 | bytes 8192 | tf_op jit(solution)/shard_map/psum | solution.py:51
  602.3 5.5 copy.14
  607.8 4.4 fusion
  612.3 1.9 copy-done.1
  614.2 11.7 %cholesky.223 = f32[128,128]{1,0:T(8,128)S(1)} custom-call(f32[128,128]{1,0:T(8,128)S(1)} %cholesky.580), custom_call_target="Cholesky" | custom-call | tf_op jit(solution)/shard_map/jit(cholesky)/cholesky | solution.py:53
  625.9 9.8 %custom-call.64 = f32[1,128,128]{1,2,0:T(8,128)S(1)} custom-call(f32[1,128,128]{2,1,0:T(8,128)S(1)} %get-tuple-element.55), custom_call_target="InvertDiagBlocksLowerTriangular" | custom-call | tf_op jit(solution)/shard_map/jit(cholesky)/cholesky | solution.py:53
  635.7 1.6 fusion.61
  637.4 1.9 convolution_subtract_fusion
  639.5 11.9 %cholesky.244 = f32[128,128]{1,0:T(8,128)S(1)} custom-call(f32[128,128]{1,0:T(8,128)S(1)} %cholesky.584), custom_call_target="Cholesky" | custom-call | tf_op jit(solution)/shard_map/jit(cholesky)/cholesky | solution.py:53
  651.4 2.5 cholesky.255
  655.4 9.8 %custom-call.65 = f32[1,128,128]{1,2,0:T(8,128)S(1)} custom-call(f32[1,128,128]{2,1,0:T(8,128)S(1)} %get-tuple-element.52), custom_call_target="InvertDiagBlocksLowerTriangular" | custom-call | tf_op jit(solution)/shard_map/jit(cholesky)/cholesky | solution.py:53
  666.5 2.1 convolution_subtract_fusion.1
  668.6 11.7 %cholesky.468 = f32[128,128]{1,0:T(8,128)S(1)} custom-call(f32[128,128]{1,0:T(8,128)S(1)} %cholesky.589), custom_call_target="Cholesky" | custom-call | tf_op jit(solution)/shard_map/jit(cholesky)/cholesky | solution.py:53
  681.6 9.8 %custom-call.66 = f32[1,128,128]{1,2,0:T(8,128)S(1)} custom-call(f32[1,128,128]{2,1,0:T(8,128)S(1)} %get-tuple-element.49), custom_call_target="InvertDiagBlocksLowerTriangular" | custom-call | tf_op jit(solution)/shard_map/jit(cholesky)/cholesky | solution.py:53
  692.6 2.3 convolution_subtract_fusion.2
  694.9 12.1 %cholesky.487 = f32[128,128]{1,0:T(8,128)S(1)} custom-call(f32[128,128]{1,0:T(8,128)S(1)} %cholesky.594), custom_call_target="Cholesky" | custom-call | tf_op jit(solution)/shard_map/jit(cholesky)/cholesky | solution.py:53
  708.4 9.8 %custom-call.67 = f32[1,128,128]{1,2,0:T(8,128)S(1)} custom-call(f32[1,128,128]{2,1,0:T(8,128)S(1)} %get-tuple-element.46), custom_call_target="InvertDiagBlocksLowerTriangular" | custom-call | tf_op jit(solution)/shard_map/jit(cholesky)/cholesky | solution.py:53
  719.3 2.3 convolution_subtract_fusion.3
  721.6 11.7 %cholesky.506 = f32[128,128]{1,0:T(8,128)S(1)} custom-call(f32[128,128]{1,0:T(8,128)S(1)} %cholesky.599), custom_call_target="Cholesky" | custom-call | tf_op jit(solution)/shard_map/jit(cholesky)/cholesky | solution.py:53
  734.6 10.0 %custom-call.68 = f32[1,128,128]{1,2,0:T(8,128)S(1)} custom-call(f32[1,128,128]{2,1,0:T(8,128)S(1)} %get-tuple-element.43), custom_call_target="InvertDiagBlocksLowerTriangular" | custom-call | tf_op jit(solution)/shard_map/jit(cholesky)/cholesky | solution.py:53
  745.7 2.3 convolution_subtract_fusion.4
  747.9 11.7 %cholesky.526 = f32[128,128]{1,0:T(8,128)S(1)} custom-call(f32[128,128]{1,0:T(8,128)S(1)} %cholesky.604), custom_call_target="Cholesky" | custom-call | tf_op jit(solution)/shard_map/jit(cholesky)/cholesky | solution.py:53
  761.0 9.8 %custom-call.69 = f32[1,128,128]{1,2,0:T(8,128)S(1)} custom-call(f32[1,128,128]{2,1,0:T(8,128)S(1)} %get-tuple-element.40), custom_call_target="InvertDiagBlocksLowerTriangular" | custom-call | tf_op jit(solution)/shard_map/jit(cholesky)/cholesky | solution.py:53
  771.7 2.0 convolution_subtract_fusion.5
  773.8 11.9 %cholesky.546 = f32[128,128]{1,0:T(8,128)S(1)} custom-call(f32[128,128]{1,0:T(8,128)S(1)} %cholesky.609), custom_call_target="Cholesky" | custom-call | tf_op jit(solution)/shard_map/jit(cholesky)/cholesky | solution.py:53
  786.9 9.8 %custom-call.70 = f32[1,128,128]{1,2,0:T(8,128)S(1)} custom-call(f32[1,128,128]{2,1,0:T(8,128)S(1)} %get-tuple-element.37), custom_call_target="InvertDiagBlocksLowerTriangular" | custom-call | tf_op jit(solution)/shard_map/jit(cholesky)/cholesky | solution.py:53
  797.6 1.8 convolution_subtract_fusion.6
  799.4 11.7 %cholesky.564 = f32[128,128]{1,0:T(8,128)S(1)} custom-call(f32[128,128]{1,0:T(8,128)S(1)} %convolution_subtract_fusion.6), custom_call_target="Cholesky" | custom-call | tf_op jit(solution)/shard_map/jit(cholesky)/cholesky | solution.py:53
  818.2 4.8 fusion.1
  823.8 27.8 %while.1 = (s32[]{:T(128)}, f32[1024,1024]{1,0:T(8,128)}, s32[8,2]{0,1:T(2,128)S(1)}, f32[8,128,128]{2,1,0:T(8,128)}, s32[]{:T(128)}) while((s32[]{:T(128)}, f32[1024,1024]{1,0:T(8,128)}, s32[8,2]{0,1:T(2,128)S(1)}, f32[8,128,128]{2,1,0:T(8,128)}, s32[]{:T(128)}) %tuple.77), condition=%wide.while_cond, body=%wide.while_body.sunk | while | flops 2 | bytes 132205 | solution.py:54
  824.4 2.9 bitcast_dynamic-update-slice_fusion.2
  827.9 2.9 bitcast_dynamic-update-slice_fusion.2
  831.4 2.9 bitcast_dynamic-update-slice_fusion.2
  834.9 2.9 bitcast_dynamic-update-slice_fusion.2
  838.4 2.9 bitcast_dynamic-update-slice_fusion.2
  841.9 2.9 bitcast_dynamic-update-slice_fusion.2
  845.3 2.9 bitcast_dynamic-update-slice_fusion.2
  848.8 2.8 bitcast_dynamic-update-slice_fusion.2
  851.6 79.6 %custom-call.71 = f32[8,128,128]{1,2,0:T(8,128)S(1)} custom-call(f32[8,128,128]{2,1,0:T(8,128)} %get-tuple-element.10), custom_call_target="InvertDiagBlocksLowerTriangular" | custom-call | tf_op jit(solution)/shard_map/triangular_solve | solution.py:54
  936.9 1.4 fusion.39
  938.5 1.4 fusion.29
  940.0 1.5 fusion.23
  951.2 1.4 fusion.25
  952.9 2.4 fusion.145
  (128 shorter events, 44.3 us)
Async XLA Ops:
  7.2 945.7 %copy-start = (f32[512,1024]{1,0:T(8,128)S(1)}, f32[512,1024]{1,0:T(8,128)}, u32[]{:S(2)}) copy-start(f32[512,1024]{1,0:T(8,128)} %param.19) | copy-start | bytes 6291460
  7.2 9.9 %copy-start.4 = (f32[8,1024]{1,0:T(8,128)S(1)}, f32[8,1024]{1,0:T(8,128)}, u32[]{:S(2)}) copy-start(f32[8,1024]{1,0:T(8,128)} %param.17) | copy-start | bytes 98308
  7.2 244.6 %all-reduce.3.cloned.1.call-start = ((), (), s32[]{:S(2)}) async-start(), calls=%async_computation | async-start | bytes 4194304 | tf_op jit(solution)/shard_map/psum | solution.py:51
  15.9 1.1 copy-start.2
  17.3 234.5 %copy-start.5 = (f32[384]{0:T(512)S(1)}, f32[384]{0:T(512)}, u32[]{:S(2)}) copy-start(f32[384]{0:T(512)} %param.13) | copy-start | bytes 4612
  17.3 234.5 %copy-start.3 = (f32[384,384]{1,0:T(8,128)S(1)}, f32[384,384]{1,0:T(8,128)}, u32[]{:S(2)}) copy-start(f32[384,384]{1,0:T(8,128)} %param.10) | copy-start | bytes 1769476
  17.3 235.2 %copy-start.6 = (f32[8]{0:T(128)S(1)}, f32[8]{0:T(128)}, u32[]{:S(2)}) copy-start(f32[8]{0:T(128)} %param.18) | copy-start | bytes 100
  23.9 578.4 %all-gather.2.cloned.1.call-start = ((), (), s32[]{:S(2)}) async-start(), calls=%async_computation.1 | async-start | bytes 6291456 | tf_op jit(solution)/shard_map/all_gather | solution.py:52
  612.2 1.9 copy-start.1
Sparse Core Ops, SparseCore 0:
  24.0 227.6 all-reduce.2
  253.5 16.5 all-gather.1
where the time goes:
time: 972 us; the launch traced here: 963 us
  blocking collectives  347 us (36%)
  other arithmetic  263 us (27%)
  waiting for transfers between devices  228 us (23%)
  matrix products  60.1 us (6%)
  local copies, waits for them, and re-layouts  44.3 us (5%)
  between operations  20 us (2%)
    psum x1, blocking collectives, per_device(): gram_sum, moment = lax.psum((gram_part, moment_part), 'rows')  347 us
    psum x1, waiting for transfers between devices, per_device(): gram_sum, moment = lax.psum((gram_part, moment_part), 'rows')  228 us
    another operation x30, other arithmetic, per_device(): lower_factor = jnp.linalg.cholesky(gram)  172 us
    another operation x3, other arithmetic, per_device(): lax.linalg.triangular_solve(lower_factor, moment[:, None], left_side=True...  84.5 us
    another operation x24, local copies, waits for them, and re-layouts  27.8 us
    another operation x14, matrix products, per_device(): lower_factor = jnp.linalg.cholesky(gram)  22.7 us
  transfers between devices with their start and end apart: 2, of which 1 were waited for; matrix products, arithmetic and copies ran while one was open for 0% of the time, Pallas kernels for 0%

commit v1 on v0

v1 whole, which is shorter than its diff:
```python
import functools

import jax
import jax.numpy as jnp
from jax import lax
from jax.experimental import pallas as pl
from jax.experimental.pallas import tpu as pltpu
from jax.sharding import PartitionSpec as P

F32, BF16 = jnp.float32, jnp.bfloat16
MESH = pl.DeviceIdType.MESH
NX, NY, NZ = 4, 4, 8
SENSORS, BALANCE, PRIOR = 384, 128, 16
DEPTH = SENSORS + BALANCE + PRIOR
NN = (((1,), (0,)), ((), ()))
NT = (((1,), (1,)), ((), ()))
TN = (((0,), (0,)), ((), ()))


def dot(a, b, dims=NN):
    return lax.dot_general(a, b, dims, preferred_element_type=F32)


def split2(x):
    hi = x.astype(BF16)
    return hi, (x - hi.astype(F32)).astype(BF16)


def split3(x):
    hi = x.astype(BF16)
    rest = x - hi.astype(F32)
    mid = rest.astype(BF16)
    return hi, mid, (rest - mid.astype(F32)).astype(BF16)


def dot3(a, b, dims=NN):
    return dot(a[0], b[0], dims) + (dot(a[0], b[1], dims) + dot(a[1], b[0], dims))


def local_kernel(w_ref, st_ref, co_ref, rd_ref, en_ref, cd_ref, br_ref, pr_ref, pi_ref, p0_ref, p1_ref, sh, sl):
    core = lax.axis_index("cols")
    w = split2(w_ref[...])
    states, coeffs, ends = st_ref[...], co_ref[...], en_ref[...]
    cond_row = cd_ref[...]
    cond = jnp.transpose(jnp.broadcast_to(cond_row, (128, 128)))
    readings = split2(jnp.broadcast_to(rd_ref[...], (8, SENSORS)))
    meas = dot3(readings, w, NT)
    right = jnp.concatenate(
        [
            meas,
            jnp.broadcast_to(cond_row * br_ref[...], (8, BALANCE)),
            jnp.broadcast_to(pi_ref[...], (8, PRIOR)),
        ],
        axis=1,
    )
    right = split2(right)
    for j in range(8):
        cols = slice(128 * j, 128 * j + 128)
        ids = 128 * j + lax.broadcasted_iota(jnp.int32, (SENSORS, 128), 1)
        h = jnp.zeros((SENSORS, 128), F32)
        for k in range(4):
            h = h + jnp.where(ids == states[:, k : k + 1], coeffs[:, k : k + 1], 0.0)
        s = dot3(w, split2(h))
        bids = ids[:BALANCE]
        bal = jnp.where(bids == ends[:, 0:1], cond, 0.0) - jnp.where(bids == ends[:, 1:2], cond, 0.0)
        pri = jnp.concatenate([pr_ref[:, cols], jnp.zeros((8, 128), F32)], axis=0)
        full = split2(jnp.concatenate([s, bal, pri], axis=0))
        sh[:, cols] = full[0]
        sl[:, cols] = full[1]
        mom = dot3(right, full)
        for a in range(4):
            p0_ref[a, 36, j : j + 1, :] = mom[0:1, :]

    def emit(pair, ref):
        for base, first in ((0, pair), (8 - pair, 7 - pair)):
            rows = slice(128 * first, 128 * first + 128)
            for j0 in range(first, 8):
                cols = slice(128 * j0, 128 * j0 + 128)
                blk = dot3((sh[:, rows], sl[:, rows]), (sh[:, cols], sl[:, cols]), TN)
                blk = blk.reshape(4, 4, 8, 128)
                at = base + j0 - first
                for a in range(4):
                    for b in range(4):
                        ref[a, b * 9 + at] = blk[a, b]

    for which in range(2):
        @pl.when(core == which)
        def _():
            emit(2 * which, p0_ref)
            emit(2 * which + 1, p1_ref)


def local_part(*args):
    vmem = pl.BlockSpec(memory_space=pltpu.VMEM)
    return pl.pallas_call(
        local_kernel,
        out_shape=(
            jax.ShapeDtypeStruct((4, 37, 8, 128), F32),
            jax.ShapeDtypeStruct((4, 36, 8, 128), F32),
        ),
        in_specs=[vmem] * len(args),
        out_specs=(vmem, vmem),
        scratch_shapes=[pltpu.VMEM((DEPTH, 1024), BF16), pltpu.VMEM((DEPTH, 1024), BF16)],
        compiler_params=pltpu.CompilerParams(vmem_limit_bytes=40 * 1024 * 1024),
    )(*args)


def sum_kernel(p0, p1, g, mom, r1a, r1b, q0, q1, r2a, r2b, zs, r3, b4, s_sem, r_sem):
    row = lax.axis_index("rows")
    core = lax.axis_index("cols")
    x, y, z = row // (NY * NZ), (row // NZ) % NY, row % NZ

    def at_x(v):
        return ((v * NY + y) * NZ + z, core)

    def at_y(v):
        return ((x * NY + v) * NZ + z, core)

    def at_z(v):
        return ((x * NY + y) * NZ + v, core)

    sibling = (row, 1 - core)
    hop = lambda v, d, n: lax.rem(v + d, n)
    barrier = pltpu.get_barrier_semaphore()
    for d in range(1, 4):
        pl.semaphore_signal(barrier, inc=1, device_id=at_x(hop(x, d, NX)), device_id_type=MESH)
        pl.semaphore_signal(barrier, inc=1, device_id=at_y(hop(y, d, NY)), device_id_type=MESH)
    for d in range(1, 8):
        pl.semaphore_signal(barrier, inc=1, device_id=at_z(hop(z, d, NZ)), device_id_type=MESH)
    pl.semaphore_signal(barrier, inc=1, device_id=sibling, device_id_type=MESH)
    pl.semaphore_wait(barrier, 14)

    copies = []
    used = [0]

    def send(src, dst, to):
        n = used[0]
        used[0] += 1
        cp = pltpu.make_async_remote_copy(
            src_ref=src, dst_ref=dst, send_sem=s_sem.at[n], recv_sem=r_sem.at[n], device_id=to, device_id_type=MESH
        )
        cp.start()
        copies.append(cp)
        return cp

    wa, wb = [], []
    for d in range(1, 4):
        to = hop(x, d, NX)
        wa.append(send(p0.at[to], r1a.at[x], at_x(to)))
        to = hop(y, d, NY)
        wb.append(send(p1.at[to], r1b.at[y], at_y(to)))
    r1a[x] = p0[x]
    r1b[y] = p1[y]
    for cp in wa:
        cp.wait_recv()
    for b in range(4):
        t = slice(9 * b, 9 * b + 9)
        q0[b, 0:9] = (r1a[0, t] + r1a[1, t]) + (r1a[2, t] + r1a[3, t])
    m = (r1a[0, 36] + r1a[1, 36]) + (r1a[2, 36] + r1a[3, 36])
    for b in range(4):
        q0[b, 9] = m
    wa = [send(q0.at[hop(y, d, NY)], r2a.at[y], at_y(hop(y, d, NY))) for d in range(1, 4)]
    for cp in wb:
        cp.wait_recv()
    for b in range(4):
        t = slice(9 * b, 9 * b + 9)
        q1[b] = (r1b[0, t] + r1b[1, t]) + (r1b[2, t] + r1b[3, t])
    wb = [send(q1.at[hop(x, d, NX)], r2b.at[x], at_x(hop(x, d, NX))) for d in range(1, 4)]
    r2a[y] = q0[y]
    r2b[x] = q1[x]
    for cp in wa:
        cp.wait_recv()
    a0 = (r2a[0] + r2a[1]) + (r2a[2] + r2a[3])
    for cp in wb:
        cp.wait_recv()
    a1 = (r2b[0] + r2b[1]) + (r2b[2] + r2b[3])
    for n in range(3):
        zs[n, 0:3] = a0[3 * n : 3 * n + 3]
        zs[3 + n, 0:3] = a1[3 * n : 3 * n + 3]
    for n in range(2):
        zs[6 + n, 0:3] = jnp.zeros((3, 8, 128), F32)
    for n in range(8):
        zs[n, 3] = a0[9]
    wz = [send(zs.at[hop(z, d, NZ)], r3.at[z], at_z(hop(z, d, NZ))) for d in range(1, 8)]
    r3[z] = zs[z]
    for cp in wz:
        cp.wait_recv()
    total = ((r3[0] + r3[1]) + (r3[2] + r3[3])) + ((r3[4] + r3[5]) + (r3[6] + r3[7]))
    mom[...] = total[3]
    b4[z] = total[0:3]
    wz = [send(b4.at[z], b4.at[z], at_z(hop(z, d, NZ))) for d in range(1, 8)]
    for cp in wz:
        cp.wait_recv()
    for n in range(3):
        g[core, 0, x, y, 3 * n : 3 * n + 3] = b4[n]
        g[core, 1, y, x, 3 * n : 3 * n + 3] = b4[3 + n]
    wa, wb = [], []
    for d in range(1, 4):
        mine = g.at[core, 0, x, y]
        wa.append(send(mine, mine, at_y(hop(y, d, NY))))
        mine = g.at[core, 1, y, x]
        wb.append(send(mine, mine, at_x(hop(x, d, NX))))
    for cp in wa:
        cp.wait_recv()
    mine = g.at[core, 0, x]
    wa = [send(mine, mine, at_x(hop(x, d, NX))) for d in range(1, 4)]
    last = [send(mine, mine, sibling)]
    for cp in wb:
        cp.wait_recv()
    mine = g.at[core, 1, y]
    wb = [send(mine, mine, at_y(hop(y, d, NY))) for d in range(1, 4)]
    last.append(send(mine, mine, sibling))
    for d in range(1, 4):
        wa[d - 1].wait_recv()
        got = g.at[core, 0, hop(x, NX - d, NX)]
        last.append(send(got, got, sibling))
        wb[d - 1].wait_recv()
        got = g.at[core, 1, hop(y, NY - d, NY)]
        last.append(send(got, got, sibling))
    for cp in last:
        cp.wait_recv()
    for cp in copies:
        cp.wait_send()


N_COPIES = 46


def sum_over_chips(p0, p1):
    vmem = pl.BlockSpec(memory_space=pltpu.VMEM)
    tiles = lambda *lead: pltpu.VMEM(lead + (8, 128), F32)
    return pl.pallas_call(
        sum_kernel,
        out_shape=(
            jax.ShapeDtypeStruct((2, 2, 4, 4, 9, 8, 128), F32),
            jax.ShapeDtypeStruct((8, 128), F32),
        ),
        in_specs=[vmem, vmem],
        out_specs=(vmem, vmem),
        scratch_shapes=[
            tiles(4, 37),
            tiles(4, 36),
            tiles(4, 10),
            tiles(4, 9),
            tiles(4, 10),
            tiles(4, 9),
            tiles(8, 4),
            tiles(8, 4),
            tiles(8, 3),
            pltpu.SemaphoreType.DMA((N_COPIES,)),
            pltpu.SemaphoreType.DMA((N_COPIES,)),
        ],
        compiler_params=pltpu.CompilerParams(
            collective_id=0, has_side_effects=True, vmem_limit_bytes=40 * 1024 * 1024
        ),
    )(p0, p1)


def bc(row, lane):
    return jnp.broadcast_to(row[:, lane : lane + 1], (1, 128))


def factor_block(ds, rd):
    lane = lax.broadcasted_iota(jnp.int32, (1, 128), 1)
    rows = [ds[s : s + 1, :] for s in range(8)]
    a = {(s, t): bc(rows[s], t) for s in range(8) for t in range(s, 8)}
    for g in range(16):
        r0 = 8 * g
        own = (lane >= r0) & (lane < r0 + 8)
        last = g == 15
        p = list(rows)
        v = [jnp.where(lane == r0 + s, 1.0, 0.0).astype(F32) for s in range(8)]
        u, w = [], []
        if not last:
            nxt = [jnp.where(own, 0.0, ds[r0 + 8 + t : r0 + 9 + t, :]) for t in range(8)]
            na = {(s, t): bc(nxt[s], r0 + 8 + t) for s in range(8) for t in range(s, 8)}
        for s in range(8):
            inv = lax.rsqrt(a[s, s])
            l = {t: a[s, t] * inv for t in range(s + 1, 8)}
            for t in range(s + 1, 8):
                for q in range(t, 8):
                    a[t, q] = a[t, q] - l[t] * l[q]
            us = p[s] * inv
            vs = v[s] * inv
            for t in range(s + 1, 8):
                p[t] = p[t] - l[t] * us
                v[t] = v[t] - l[t] * vs
            ws = jnp.where(own, vs, us)
            u.append(us)
            w.append(ws)
            rd[r0 + s : r0 + s + 1, :] = jnp.where(lane >= r0 + s, us, 0.0)
            ds[r0 + s : r0 + s + 1, :] = jnp.where(lane < r0 + 8, ws, 0.0)
            if not last:
                m = [bc(us, r0 + 8 + t) for t in range(8)]
                for t in range(8):
                    nxt[t] = nxt[t] - m[t] * ws
                    for q in range(t, 8):
                        na[t, q] = na[t, q] - m[t] * m[q]
        if not last:
            rows, a = nxt, na
        if g < 14:
            uh, um, ul = split3(jnp.concatenate(u, axis=0))
            wh, wm, wl = split3(jnp.concatenate(w, axis=0))
            lhs = jnp.concatenate([uh, uh, um, uh, ul, um], axis=0)
            rhs = jnp.concatenate([wh, wm, wh, wl, wh, wm], axis=0)
            upd = dot(lhs, rhs, TN)
            t0 = r0 + 16
            ds[t0:, :] = jnp.where(own, 0.0, ds[t0:, :]) - upd[t0:, :]


def solve_kernel(g_ref, m_ref, t_ref, r_ref, z_ref, x_ref, a_s, ds, rd, di_s, rp_s, zv, t_s, g_sem, t_sem):
    row_id = lax.axis_index("rows")
    core = lax.axis_index("cols")
    loads = []
    for bi in range(8):
        pair = min(bi, 7 - bi)
        base = 0 if bi < 4 else 8 - pair
        for bj in range(bi, 8):
            cp = pltpu.make_async_copy(
                g_ref.at[pair, :, base + bj - bi], a_s.at[bi, :, :, pl.ds(128 * bj, 128)], g_sem.at[bi, bj]
            )
            cp.start()
            loads.append(cp)
    t_load = pltpu.make_async_copy(t_ref, t_s, t_sem)
    t_load.start()
    for i in range(8):
        col = jnp.transpose(jnp.broadcast_to(m_ref[i : i + 1, :], (128, 128)))
        a_s[i, :, :, 1024:] = col.reshape(16, 8, 128)
    for cp in loads:
        cp.wait()

    def block(i, j):
        return a_s[i, :, :, pl.ds(pl.multiple_of(j * 128, 128), 128)].reshape(128, 128)

    def put(i, j, val):
        a_s[i, :, :, pl.ds(pl.multiple_of(j * 128, 128), 128)] = val.reshape(16, 8, 128)

    def panel(k, _):
        ds[...] = block(k, k)
        factor_block(ds, rd)
        di = ds[...]
        di_s[k] = di
        dh, dl = split2(di)
        dcat = jnp.concatenate([dh, dl, dh], axis=1)

        def col(j, _):
            cols = pl.ds(pl.multiple_of(j * 128, 128), 128)
            ah, al = split2(block(k, j))
            r = dot(dcat, jnp.concatenate([ah, ah, al], axis=0))
            put(k, j, r)
            rh, rl = split2(r)
            rp_s[0:128, cols] = rh
            rp_s[128:256, cols] = rh
            rp_s[256:384, cols] = rl
            return 0

        lax.fori_loop(k + 1, 9, col, 0)
        put(k, k, rd[...])

        def trail(i, _):
            th, tl = split2(jnp.transpose(block(k, i)))
            lhs = jnp.concatenate([th, tl, th], axis=1)

            def one(j, _):
                cols = pl.ds(pl.multiple_of(j * 128, 128), 128)
                put(i, j, block(i, j) - dot(lhs, rp_s[:, cols]))
                return 0

            lax.fori_loop(i, 9, one, 0)
            return 0

        lax.fori_loop(k + 1, 8, trail, 0)
        return 0

    lax.fori_loop(0, 8, panel, 0)

    y = [jnp.transpose(block(i, 8))[0:8, :] for i in range(8)]
    for i in range(8):
        zv[i : i + 1, :] = y[i][0:1, :]
    z_ref[...] = zv[pl.ds(core * 4, 4), :]
    e = [None] * 8
    for k in range(7, -1, -1):
        e[k] = dot3(split2(y[k]), split2(di_s[k]))
        if k:
            r = a_s[0:k, :, :, 128 * k : 128 * k + 128].reshape(128 * k, 128)
            upd = dot3(split2(e[k]), split2(r), NT)
            for p in range(k):
                y[p] = y[p] - upd[:, 128 * p : 128 * p + 128]
    t_load.wait()
    x = dot3(split2(jnp.concatenate(e, axis=1)), split2(t_s[...]), NT)
    x_ref[...] = x[0:1, :]
    mine = a_s[row_id // 16, row_id % 16, :, pl.ds(pl.multiple_of(core * 512, 512), 512)]
    at_row = row_id * 8 + lax.broadcasted_iota(jnp.int32, (8, 512), 0)
    at_col = core * 512 + lax.broadcasted_iota(jnp.int32, (8, 512), 1)
    r_ref[...] = jnp.where(at_col >= at_row, mine, 0.0)


def solve(g, m, t):
    vmem = pl.BlockSpec(memory_space=pltpu.VMEM)
    hbm = pl.BlockSpec(memory_space=pl.ANY)
    return pl.pallas_call(
        solve_kernel,
        out_shape=(
            jax.ShapeDtypeStruct((8, 512), F32),
            jax.ShapeDtypeStruct((4, 128), F32),
            jax.ShapeDtypeStruct((1, 512), F32),
        ),
        in_specs=[hbm, vmem, hbm],
        out_specs=(vmem, vmem, vmem),
        scratch_shapes=[
            pltpu.VMEM((8, 16, 8, 1152), F32),
            pltpu.VMEM((128, 128), F32),
            pltpu.VMEM((128, 128), F32),
            pltpu.VMEM((8, 128, 128), F32),
            pltpu.VMEM((384, 1152), BF16),
            pltpu.VMEM((8, 128), F32),
            pltpu.VMEM((512, 1024), F32),
            pltpu.SemaphoreType.DMA((8, 8)),
            pltpu.SemaphoreType.DMA,
        ],
        compiler_params=pltpu.CompilerParams(vmem_limit_bytes=40 * 1024 * 1024),
    )(g, m, t)


def per_device(
    whitening,
    sensor_states,
    sensor_coefficients,
    sensor_readings,
    conduit_endpoints,
    conductance,
    balance_right_side,
    prior_root_factor,
    prior_information,
    transition,
):
    prior_row = jnp.concatenate([prior_information, jnp.zeros((PRIOR - 8,), F32)])
    p0, p1 = local_part(
        whitening,
        sensor_states,
        sensor_coefficients,
        sensor_readings.reshape(1, SENSORS),
        conduit_endpoints,
        conductance.reshape(1, BALANCE),
        balance_right_side.reshape(1, BALANCE),
        prior_root_factor,
        prior_row.reshape(1, PRIOR),
    )
    g, moment = sum_over_chips(p0, p1)
    r_post, z_post, x_next = solve(g.reshape(4, 16, 9, 8, 128), moment, transition)
    return r_post, z_post.reshape(512), x_next.reshape(512)


def solution(mesh):
    in_specs = (
        P("rows", None),
        P("rows", None),
        P("rows", None),
        P("rows"),
        P("rows", None),
        P("rows"),
        P("rows"),
        P("rows", None),
        P("rows"),
        P("cols", None),
    )
    out_specs = (P("rows", "cols"), P("cols"), P("cols"))
    return jax.shard_map(
        per_device, mesh=mesh, in_specs=in_specs, out_specs=out_specs, check_vma=False
    )
```

time: 972 us -> 134 us (0.14)
  the two profiles are of different devices: /device:TPU:0 before, /device:TPU:1 now
where the time goes in v1:
time: 134 us; the launch traced here: 133 us
  Pallas kernels  125 us (93%)
  local copies, waits for them, and re-layouts  7.05 us (5%)
    pallas_call x1, Pallas kernels, solve(): pl.pallas_call(solve_kernel, out_shape=(jax.ShapeDtypeStruct((8, 512), F3...  68.3 us
    pallas_call x1, Pallas kernels, sum_over_chips(): pl.pallas_call(sum_kernel, out_shape=(jax.ShapeDtypeStruct((2, 2, 4, 4, 9...  49.8 us
    pallas_call x1, Pallas kernels, local_part(): pl.pallas_call(local_kernel, out_shape=(jax.ShapeDtypeStruct((4, 37, 8, 1...  7.33 us
    unnamed x13, local copies, waits for them, and re-layouts  5.56 us

profile of v1, /device:TPU:1, one launch (start us, length us, event | category | flops | bytes accessed | tf_op | source)
XLA Modules:
  0.0 133.4 jit_solution(1232092078060963198)
XLA Ops:
  0.6 0.0 copy-start
  0.6 0.8 pad_bitcast_fusion.pi_ref
  1.4 0.7 reshape.27.rd_ref
  2.1 0.8 copy.15.en_ref
  2.9 0.8 copy.13.st_ref
  3.7 0.8 copy.14.co_ref
  4.6 0.0 copy-start.1
  4.6 1.1 copy-done.1
  5.6 0.0 copy-start.2
  5.7 0.8 copy-done.2
  6.4 0.0 copy-start.3
  6.4 0.7 copy-done.3
  7.1 0.0 copy-start.4
  7.1 0.7 copy-done.4
  7.7 7.3 %shard_map.121 = (f32[4,37,8,128]{3,2,1,0:T(8,128)S(1)}, f32[4,36,8,128]{3,2,1,0:T(8,128)S(1)}) custom-call(f32[384,384]{1,0:T(8,128)S(1)} %copy-done.1, s32[384,4]{1,0:T(8,128)S(1)} %copy.13.st_ref, f32[384,4]{1,0:T(8,128)S(1)} %copy.14.co_ref, f32[1,384]{1,0:T(1,128)S(1)} %reshape.27.rd_ref, s32[128,2]{1,0:T(8,128)S(1)} %copy.15.en_ref, ...), custom_call_target="tpu_custom_call" | custom-call | tf_op jit(solution)/shard_map/pallas_call | solution.py:95
  15.1 49.8 %shard_map.122 = (f32[2,2,4,4,9,8,128]{6,5,4,3,2,1,0:T(8,128)S(1)}, f32[8,128]{1,0:T(8,128)S(1)}) custom-call(f32[4,37,8,128]{3,2,1,0:T(8,128)S(1)} %get-tuple-element.10.p0, f32[4,36,8,128]{3,2,1,0:T(8,128)S(1)} %get-tuple-element.11.p1), custom_call_target="tpu_custom_call" | custom-call | tf_op jit(solution)/shard_map/pallas_call | solution.py:232
  64.9 0.0 copy-done
  64.9 68.3 %shard_map.123 = (f32[8,512]{1,0:T(8,128)}, f32[4,128]{1,0:T(4,128)}, f32[1,512]{1,0:T(1,128)}) custom-call(f32[4,16,9,8,128]{4,3,2,1,0:T(8,128)S(1)} %bitcast.7, f32[8,128]{1,0:T(8,128)S(1)} %get-tuple-element.13.m_ref, f32[512,1024]{1,0:T(8,128)S(1)} %copy-done), custom_call_target="tpu_custom_call" | custom-call | tf_op jit(solution)/shard_map/pallas_call | solution.py:401
Async XLA Ops:
  0.6 64.3 %copy-start = (f32[512,1024]{1,0:T(8,128)S(1)}, f32[512,1024]{1,0:T(8,128)}, u32[]{:S(2)}) copy-start(f32[512,1024]{1,0:T(8,128)} %t_ref.1) | copy-start | bytes 6291460
  4.6 1.1 copy-start.1
  5.6 0.8 copy-start.2
  6.4 0.7 copy-start.3
  7.1 0.7 copy-start.4

commit v2 on v1

--- a/solution.py
+++ b/solution.py
@@ -10,8 +10,7 @@
 F32, BF16 = jnp.float32, jnp.bfloat16
 MESH = pl.DeviceIdType.MESH
 NX, NY, NZ = 4, 4, 8
-SENSORS, BALANCE, PRIOR = 384, 128, 16
-DEPTH = SENSORS + BALANCE + PRIOR
+SENSORS, BALANCE = 384, 128
 NN = (((1,), (0,)), ((), ()))
 NT = (((1,), (1,)), ((), ()))
 TN = (((0,), (0,)), ((), ()))
@@ -37,51 +36,71 @@
     return dot(a[0], b[0], dims) + (dot(a[0], b[1], dims) + dot(a[1], b[0], dims))
 
 
-def local_kernel(w_ref, st_ref, co_ref, rd_ref, en_ref, cd_ref, br_ref, pr_ref, pi_ref, p0_ref, p1_ref, sh, sl):
+def local_kernel(
+    w_in, st_in, co_in, rd_in, en_in, cd_in, br_in, pr_in, pi_in, p0_ref, p1_ref,
+    w_ref, st_ref, co_ref, rd_ref, en_ref, cd_ref, br_ref, pr_ref, pi_ref, sf, sr, sp, sem,
+):
     core = lax.axis_index("cols")
+    pairs = [
+        (st_in, st_ref), (co_in, co_ref), (en_in, en_ref), (cd_in, cd_ref), (br_in, br_ref),
+        (pr_in, pr_ref), (pi_in, pi_ref), (rd_in, rd_ref), (w_in, w_ref),
+    ]
+    loads = [pltpu.make_async_copy(x, y, sem.at[n]) for n, (x, y) in enumerate(pairs)]
+    for cp in loads:
+        cp.start()
+    for cp in loads:
+        cp.wait()
     w = split2(w_ref[...])
-    states, coeffs, ends = st_ref[...], co_ref[...], en_ref[...]
+    wcat = jnp.concatenate([w[0], w[1], w[0]], axis=1)
+    spread = lambda row: jnp.transpose(jnp.broadcast_to(row, (128, 128)))
     cond_row = cd_ref[...]
-    cond = jnp.transpose(jnp.broadcast_to(cond_row, (128, 128)))
-    readings = split2(jnp.broadcast_to(rd_ref[...], (8, SENSORS)))
-    meas = dot3(readings, w, NT)
-    right = jnp.concatenate(
-        [
-            meas,
-            jnp.broadcast_to(cond_row * br_ref[...], (8, BALANCE)),
-            jnp.broadcast_to(pi_ref[...], (8, PRIOR)),
-        ],
-        axis=1,
-    )
-    right = split2(right)
+    cond = spread(cond_row)
+    ends = [spread(en_ref[k : k + 1, :].astype(F32)).astype(jnp.int32) for k in range(2)]
+    info = jnp.concatenate([pi_ref[...], jnp.zeros((1, 120), F32)], axis=1)
+    info = spread(info)[0:8, :]
+    readings = jnp.concatenate([rd_ref[k : k + 1, :] for k in range(3)], axis=1)
+    meas = dot3(split2(jnp.broadcast_to(readings, (8, SENSORS))), w, NT)
+    right = split2(jnp.concatenate([meas, jnp.broadcast_to(cond_row * br_ref[...], (8, BALANCE))], axis=1))
+    rcat = jnp.concatenate([right[0], right[1], right[0]], axis=1)
     for j in range(8):
         cols = slice(128 * j, 128 * j + 128)
-        ids = 128 * j + lax.broadcasted_iota(jnp.int32, (SENSORS, 128), 1)
-        h = jnp.zeros((SENSORS, 128), F32)
+        ids = 128 * j + lax.broadcasted_iota(jnp.int32, (128, SENSORS), 0)
+        h = jnp.zeros((128, SENSORS), F32)
         for k in range(4):
-            h = h + jnp.where(ids == states[:, k : k + 1], coeffs[:, k : k + 1], 0.0)
-        s = dot3(w, split2(h))
-        bids = ids[:BALANCE]
-        bal = jnp.where(bids == ends[:, 0:1], cond, 0.0) - jnp.where(bids == ends[:, 1:2], cond, 0.0)
-        pri = jnp.concatenate([pr_ref[:, cols], jnp.zeros((8, 128), F32)], axis=0)
-        full = split2(jnp.concatenate([s, bal, pri], axis=0))
-        sh[:, cols] = full[0]
-        sl[:, cols] = full[1]
-        mom = dot3(right, full)
+            h = h + jnp.where(ids == st_ref[k : k + 1, :], co_ref[k : k + 1, :], 0.0)
+        hh, hl = split2(h)
+        s = dot(wcat, jnp.concatenate([hh, hh, hl], axis=1), NT)
+        bids = 128 * j + lax.broadcasted_iota(jnp.int32, (BALANCE, 128), 1)
+        bal = jnp.where(bids == ends[0], cond, 0.0) - jnp.where(bids == ends[1], cond, 0.0)
+        full = jnp.concatenate([s, bal], axis=0)
+        sf[:, cols] = full
+        fh, fl = split2(full)
+        sr[0:512, cols] = fh
+        sr[512:1024, cols] = fh
+        sr[1024:1536, cols] = fl
+        prior = pr_ref[:, cols]
+        ph, pm, pl_ = split3(prior)
+        sp[0, :, cols] = jnp.concatenate([ph, ph, pm, ph, pl_, pm], axis=0)
+        sp[1, :, cols] = jnp.concatenate([ph, pm, ph, pl_, ph, pm], axis=0)
+        mom = dot(rcat, sr[:, cols])[0:1, :] + jnp.sum(prior * info, axis=0, keepdims=True)
         for a in range(4):
-            p0_ref[a, 36, j : j + 1, :] = mom[0:1, :]
+            p0_ref[a, 36, j : j + 1, :] = mom
 
     def emit(pair, ref):
         for base, first in ((0, pair), (8 - pair, 7 - pair)):
             rows = slice(128 * first, 128 * first + 128)
-            for j0 in range(first, 8):
-                cols = slice(128 * j0, 128 * j0 + 128)
-                blk = dot3((sh[:, rows], sl[:, rows]), (sh[:, cols], sl[:, cols]), TN)
-                blk = blk.reshape(4, 4, 8, 128)
-                at = base + j0 - first
-                for a in range(4):
-                    for b in range(4):
-                        ref[a, b * 9 + at] = blk[a, b]
+            th, tl = split2(jnp.concatenate([jnp.transpose(sf[128 * n : 128 * n + 128, rows]) for n in range(4)], axis=1))
+            lhs = jnp.concatenate([th, tl, th], axis=1)
+            for j0 in range(first, 8, 2):
+                j1 = min(j0 + 2, 8)
+                cols = slice(128 * j0, 128 * j1)
+                wide = dot(lhs, sr[:, cols]) + dot(sp[0, :, rows], sp[1, :, cols], TN)
+                for j in range(j0, j1):
+                    blk = wide[:, 128 * (j - j0) : 128 * (j - j0) + 128].reshape(4, 4, 8, 128)
+                    at = base + j - first
+                    for a in range(4):
+                        for b in range(4):
+                            ref[a, b * 9 + at] = blk[a, b]
 
     for which in range(2):
         @pl.when(core == which)
@@ -98,10 +117,16 @@
             jax.ShapeDtypeStruct((4, 37, 8, 128), F32),
             jax.ShapeDtypeStruct((4, 36, 8, 128), F32),
         ),
-        in_specs=[vmem] * len(args),
+        in_specs=[pl.BlockSpec(memory_space=pltpu.HBM)] * len(args),
         out_specs=(vmem, vmem),
-        scratch_shapes=[pltpu.VMEM((DEPTH, 1024), BF16), pltpu.VMEM((DEPTH, 1024), BF16)],
-        compiler_params=pltpu.CompilerParams(vmem_limit_bytes=40 * 1024 * 1024),
+        scratch_shapes=[pltpu.VMEM(x.shape, x.dtype) for x in args]
+        + [
+            pltpu.VMEM((512, 1024), F32),
+            pltpu.VMEM((1536, 1024), BF16),
+            pltpu.VMEM((2, 48, 1024), BF16),
+            pltpu.SemaphoreType.DMA((9,)),
+        ],
+        compiler_params=pltpu.CompilerParams(vmem_limit_bytes=62 * 1024 * 1024),
     )(*args)
 
 
@@ -251,64 +276,67 @@
             pltpu.SemaphoreType.DMA((N_COPIES,)),
         ],
         compiler_params=pltpu.CompilerParams(
-            collective_id=0, has_side_effects=True, vmem_limit_bytes=40 * 1024 * 1024
+            collective_id=0, has_side_effects=True, vmem_limit_bytes=62 * 1024 * 1024
         ),
     )(p0, p1)
 
 
-def bc(row, lane):
-    return jnp.broadcast_to(row[:, lane : lane + 1], (1, 128))
-
-
-def factor_block(ds, rd):
-    lane = lax.broadcasted_iota(jnp.int32, (1, 128), 1)
-    rows = [ds[s : s + 1, :] for s in range(8)]
-    a = {(s, t): bc(rows[s], t) for s in range(8) for t in range(s, 8)}
+def lane_bc(x, lane):
+    return jnp.broadcast_to(x[:, lane : lane + 1], (8, 128))
+
+
+def row_bc(x, row):
+    return jnp.broadcast_to(x[row : row + 1, :], (8, 128))
+
+
+def factor_block(ds, rd, lt):
+    lane = lax.broadcasted_iota(jnp.int32, (8, 128), 1)
+    sub = lax.broadcasted_iota(jnp.int32, (8, 128), 0)
+    t = [ds[8 * j : 8 * j + 8, :] for j in range(16)]
+    c = [lane_bc(t[0], q) for q in range(8)]
     for g in range(16):
         r0 = 8 * g
         own = (lane >= r0) & (lane < r0 + 8)
-        last = g == 15
-        p = list(rows)
-        v = [jnp.where(lane == r0 + s, 1.0, 0.0).astype(F32) for s in range(8)]
-        u, w = [], []
-        if not last:
-            nxt = [jnp.where(own, 0.0, ds[r0 + 8 + t : r0 + 9 + t, :]) for t in range(8)]
-            na = {(s, t): bc(nxt[s], r0 + 8 + t) for s in range(8) for t in range(s, 8)}
+        below = range(g + 1, 16)
+        b = {j: [lane_bc(t[j], r0 + q) for q in range(8)] for j in below}
+        if g < 15:
+            nc = [lane_bc(t[g + 1], r0 + 8 + q) for q in range(8)]
+        p = jnp.where(own, jnp.where(lane - r0 == sub, 1.0, 0.0), t[g])
+        for j in below:
+            t[j] = jnp.where(own, 0.0, t[j])
+        w = []
+        low = jnp.zeros((8, 128), F32)
         for s in range(8):
-            inv = lax.rsqrt(a[s, s])
-            l = {t: a[s, t] * inv for t in range(s + 1, 8)}
-            for t in range(s + 1, 8):
-                for q in range(t, 8):
-                    a[t, q] = a[t, q] - l[t] * l[q]
-            us = p[s] * inv
-            vs = v[s] * inv
-            for t in range(s + 1, 8):
-                p[t] = p[t] - l[t] * us
-                v[t] = v[t] - l[t] * vs
-            ws = jnp.where(own, vs, us)
-            u.append(us)
+            inv = lax.rsqrt(row_bc(c[s], s))
+            col = c[s] * inv
+            mult = {q: row_bc(col, q) for q in range(s + 1, 8)}
+            for q in range(s + 1, 8):
+                c[q] = c[q] - col * mult[q]
+            ws = row_bc(p, s) * inv
+            if s < 7:
+                p = p - col * ws
+            low = jnp.where(lane == r0 + s, col, low)
+            for j in below:
+                m = b[j][s] * inv
+                for q in range(s + 1, 8):
+                    b[j][q] = b[j][q] - m * mult[q]
+                t[j] = t[j] - m * ws
+                if j == g + 1:
+                    for q in range(8):
+                        nc[q] = nc[q] - m * row_bc(m, q)
             w.append(ws)
-            rd[r0 + s : r0 + s + 1, :] = jnp.where(lane >= r0 + s, us, 0.0)
-            ds[r0 + s : r0 + s + 1, :] = jnp.where(lane < r0 + 8, ws, 0.0)
-            if not last:
-                m = [bc(us, r0 + 8 + t) for t in range(8)]
-                for t in range(8):
-                    nxt[t] = nxt[t] - m[t] * ws
-                    for q in range(t, 8):
-                        na[t, q] = na[t, q] - m[t] * m[q]
-        if not last:
-            rows, a = nxt, na
-        if g < 14:
-            uh, um, ul = split3(jnp.concatenate(u, axis=0))
-            wh, wm, wl = split3(jnp.concatenate(w, axis=0))
-            lhs = jnp.concatenate([uh, uh, um, uh, ul, um], axis=0)
-            rhs = jnp.concatenate([wh, wm, wh, wl, wh, wm], axis=0)
-            upd = dot(lhs, rhs, TN)
-            t0 = r0 + 16
-            ds[t0:, :] = jnp.where(own, 0.0, ds[t0:, :]) - upd[t0:, :]
-
-
-def solve_kernel(g_ref, m_ref, t_ref, r_ref, z_ref, x_ref, a_s, ds, rd, di_s, rp_s, zv, t_s, g_sem, t_sem):
+        full = w[0]
+        for s in range(1, 8):
+            full = jnp.where(sub == s, w[s], full)
+        rd[r0 : r0 + 8, :] = jnp.where(lane >= r0 + 8, full, 0.0)
+        ds[r0 : r0 + 8, :] = jnp.where(lane < r0 + 8, full, 0.0)
+        lt[r0 : r0 + 8, :] = low
+        if g < 15:
+            c = nc
+    rd[...] = rd[...] + jnp.transpose(lt[...])
+
+
+def solve_kernel(g_ref, m_ref, t_ref, r_ref, z_ref, x_ref, a_s, ds, rd, lt, di_s, rp_s, zv, t_s, g_sem, t_sem):
     row_id = lax.axis_index("rows")
     core = lax.axis_index("cols")
     loads = []
@@ -330,46 +358,49 @@
         cp.wait()
 
     def block(i, j):
-        return a_s[i, :, :, pl.ds(pl.multiple_of(j * 128, 128), 128)].reshape(128, 128)
+        at = slice(128 * j, 128 * j + 128) if isinstance(j, int) else pl.ds(pl.multiple_of(j * 128, 128), 128)
+        return a_s[i, :, :, at].reshape(128, 128)
 
     def put(i, j, val):
         a_s[i, :, :, pl.ds(pl.multiple_of(j * 128, 128), 128)] = val.reshape(16, 8, 128)
 
     def panel(k, _):
         ds[...] = block(k, k)
-        factor_block(ds, rd)
+        factor_block(ds, rd, lt)
         di = ds[...]
         di_s[k] = di
         dh, dl = split2(di)
         dcat = jnp.concatenate([dh, dl, dh], axis=1)
 
-        def col(j, _):
-            cols = pl.ds(pl.multiple_of(j * 128, 128), 128)
-            ah, al = split2(block(k, j))
+        def columns(first):
+            cols = slice(128 * first, 1152)
+            ah, al = split2(a_s[k, :, :, cols].reshape(128, -1))
             r = dot(dcat, jnp.concatenate([ah, ah, al], axis=0))
-            put(k, j, r)
+            a_s[k, :, :, cols] = r.reshape(16, 8, -1)
             rh, rl = split2(r)
             rp_s[0:128, cols] = rh
             rp_s[128:256, cols] = rh
             rp_s[256:384, cols] = rl
-            return 0
-
-        lax.fori_loop(k + 1, 9, col, 0)
+
+        @pl.when(k < 4)
+        def _():
+            columns(1)
+
+        @pl.when(k >= 4)
+        def _():
+            columns(5)
+
         put(k, k, rd[...])
 
-        def trail(i, _):
-            th, tl = split2(jnp.transpose(block(k, i)))
-            lhs = jnp.concatenate([th, tl, th], axis=1)
-
-            def one(j, _):
-                cols = pl.ds(pl.multiple_of(j * 128, 128), 128)
-                put(i, j, block(i, j) - dot(lhs, rp_s[:, cols]))
-                return 0
-
-            lax.fori_loop(i, 9, one, 0)
-            return 0
-
-        lax.fori_loop(k + 1, 8, trail, 0)
+        for i in range(1, 8):
+
+            @pl.when(i > k)
+            def _():
+                cols = slice(128 * i, 1152)
+                th, tl = split2(jnp.transpose(block(k, i)))
+                lhs = jnp.concatenate([th, tl, th], axis=1)
+                a_s[i, :, :, cols] = a_s[i, :, :, cols] - dot(lhs, rp_s[:, cols]).reshape(16, 8, -1)
+
         return 0
 
     lax.fori_loop(0, 8, panel, 0)
@@ -397,7 +428,7 @@
 
 def solve(g, m, t):
     vmem = pl.BlockSpec(memory_space=pltpu.VMEM)
-    hbm = pl.BlockSpec(memory_space=pl.ANY)
+    hbm = pl.BlockSpec(memory_space=pltpu.HBM)
     return pl.pallas_call(
         solve_kernel,
         out_shape=(
@@ -405,10 +436,11 @@
             jax.ShapeDtypeStruct((4, 128), F32),
             jax.ShapeDtypeStruct((1, 512), F32),
         ),
-        in_specs=[hbm, vmem, hbm],
+        in_specs=[pl.BlockSpec(memory_space=pl.ANY), vmem, hbm],
         out_specs=(vmem, vmem, vmem),
         scratch_shapes=[
             pltpu.VMEM((8, 16, 8, 1152), F32),
+            pltpu.VMEM((128, 128), F32),
             pltpu.VMEM((128, 128), F32),
             pltpu.VMEM((128, 128), F32),
             pltpu.VMEM((8, 128, 128), F32),
@@ -418,7 +450,7 @@
             pltpu.SemaphoreType.DMA((8, 8)),
             pltpu.SemaphoreType.DMA,
         ],
-        compiler_params=pltpu.CompilerParams(vmem_limit_bytes=40 * 1024 * 1024),
+        compiler_params=pltpu.CompilerParams(vmem_limit_bytes=62 * 1024 * 1024),
     )(g, m, t)
 
 
@@ -434,17 +466,16 @@
     prior_information,
     transition,
 ):
-    prior_row = jnp.concatenate([prior_information, jnp.zeros((PRIOR - 8,), F32)])
     p0, p1 = local_part(
         whitening,
-        sensor_states,
-        sensor_coefficients,
-        sensor_readings.reshape(1, SENSORS),
-        conduit_endpoints,
+        sensor_states.T,
+        sensor_coefficients.T,
+        sensor_readings.reshape(3, 128),
+        conduit_endpoints.T,
         conductance.reshape(1, BALANCE),
         balance_right_side.reshape(1, BALANCE),
         prior_root_factor,
-        prior_row.reshape(1, PRIOR),
+        prior_information.reshape(1, 8),
     )
     g, moment = sum_over_chips(p0, p1)
     r_post, z_post, x_next = solve(g.reshape(4, 16, 9, 8, 128), moment, transition)

time: 134 us -> 103 us (0.77)
  Pallas kernels: 125 us -> 103 us
  local copies, waits for them, and re-layouts: 7.05 us -> 0 us
    pallas_call x1, Pallas kernels: 68.3 us -> 40.2 us  [solve(): pl.pallas_call(solve_kernel, out_shape=(jax.ShapeDtypeStruct((8, 512), F3...]
    unnamed x13 -> x0, local copies, waits for them, and re-layouts: 5.56 us -> none
    pallas_call x1, Pallas kernels: 7.33 us -> 9.98 us  [local_part(): pl.pallas_call(local_kernel, out_shape=(jax.ShapeDtypeStruct((4, 37, 8, 1...]
    pallas_call x1, Pallas kernels: 49.8 us -> 52.4 us  [sum_over_chips(): pl.pallas_call(sum_kernel, out_shape=(jax.ShapeDtypeStruct((2, 2, 4, 4, 9...]
    reshape x2 -> x0, local copies, waits for them, and re-layouts: 1.49 us -> none  [the longest x1 0.81 us: per_device(): prior_row.reshape(1, PRIOR)]
where the time goes in v2:
time: 103 us
  Pallas kernels  103 us (100%)
    pallas_call x1, Pallas kernels, sum_over_chips(): pl.pallas_call(sum_kernel, out_shape=(jax.ShapeDtypeStruct((2, 2, 4, 4, 9...  52.4 us
    pallas_call x1, Pallas kernels, solve(): pl.pallas_call(solve_kernel, out_shape=(jax.ShapeDtypeStruct((8, 512), F3...  40.2 us
    pallas_call x1, Pallas kernels, local_part(): pl.pallas_call(local_kernel, out_shape=(jax.ShapeDtypeStruct((4, 37, 8, 1...  9.98 us

profile of v2, /device:TPU:1, one launch (start us, length us, event | category | flops | bytes accessed | tf_op | source)
XLA Modules:
  0.0 103.3 jit_solution(15897390529878820813)
XLA Ops:
  0.6 10.0 %shard_map.121 = (f32[4,37,8,128]{3,2,1,0:T(8,128)}, f32[4,36,8,128]{3,2,1,0:T(8,128)}) custom-call(f32[384,384]{1,0:T(8,128)} %w_in.1, s32[4,384]{1,0:T(4,128)} %bitcast.11, f32[4,384]{1,0:T(4,128)} %bitcast.12, f32[3,128]{1,0:T(4,128)} %bitcast.13, s32[2,128]{1,0:T(2,128)} %bitcast.14, f32[1,128]{1,0:T(1,128)} %bitcast.15, f32[1,128]{1,0:T(1,128)} %bitcast.16, ...), custom_call_target="tpu_custom_call" | custom-call | tf_op jit(solution)/shard_map/pallas_call | solution.py:114
  10.6 52.4 %shard_map.122 = (f32[2,2,4,4,9,8,128]{6,5,4,3,2,1,0:T(8,128)}, f32[8,128]{1,0:T(8,128)}) custom-call(f32[4,37,8,128]{3,2,1,0:T(8,128)} %get-tuple-element.10.p0, f32[4,36,8,128]{3,2,1,0:T(8,128)} %get-tuple-element.11.p1), custom_call_target="tpu_custom_call" | custom-call | tf_op jit(solution)/shard_map/pallas_call | solution.py:257
  63.0 40.2 %shard_map.123 = (f32[8,512]{1,0:T(8,128)}, f32[4,128]{1,0:T(4,128)}, f32[1,512]{1,0:T(1,128)}) custom-call(f32[4,16,9,8,128]{4,3,2,1,0:T(8,128)} %bitcast.10, f32[8,128]{1,0:T(8,128)} %get-tuple-element.13.m_ref, f32[512,1024]{1,0:T(8,128)} %t_ref.1), custom_call_target="tpu_custom_call" | custom-call | tf_op jit(solution)/shard_map/pallas_call | solution.py:432

commit v3 on v0

v3 whole, which is shorter than its diff:
```python
import jax
import jax.numpy as jnp
from jax import lax
from jax.experimental import pallas as pl
from jax.experimental.pallas import tpu as pltpu
from jax.sharding import PartitionSpec as P

F32, BF16 = jnp.float32, jnp.bfloat16
MESH = pl.DeviceIdType.MESH
NX, NY, NZ = 4, 4, 8
SENSORS, BALANCE = 384, 128
DEPTH = 3 * (SENSORS + BALANCE) + 128
FIRST = [0, 8, 15, 21, 26, 30, 33, 35, 36]
NN = (((1,), (0,)), ((), ()))
NT = (((1,), (1,)), ((), ()))
TN = (((0,), (0,)), ((), ()))


def dot(a, b, dims=NN):
    return lax.dot_general(a, b, dims, preferred_element_type=F32)


def split2(x):
    hi = x.astype(BF16)
    return hi, (x - hi.astype(F32)).astype(BF16)


def split3(x):
    hi = x.astype(BF16)
    rest = x - hi.astype(F32)
    mid = rest.astype(BF16)
    return hi, mid, (rest - mid.astype(F32)).astype(BF16)


def dot3(a, b, dims=NN):
    return dot(a[0], b[0], dims) + (dot(a[0], b[1], dims) + dot(a[1], b[0], dims))


def spread(row):
    return jnp.transpose(jnp.broadcast_to(row, (128, 128)))


def build_rows(w_ref, st_ref, co_ref, rd_ref, en_ref, cd_ref, br_ref, pr_ref, pi_ref, wcat, hcat, sr, prt, p0, p1):
    w = split2(w_ref[...])
    wcat[...] = jnp.concatenate([w[0], w[1], w[0]], axis=1)
    cond_row = cd_ref[...]
    cond = spread(cond_row)
    ends = [spread(en_ref[k : k + 1, :].astype(F32)).astype(jnp.int32) for k in range(2)]
    info = spread(jnp.concatenate([pi_ref[...], jnp.zeros((1, 120), F32)], axis=1))[0:8, :]
    readings = jnp.concatenate([rd_ref[k : k + 1, :] for k in range(3)], axis=1)
    meas = dot3(split2(jnp.broadcast_to(readings, (8, SENSORS))), w, NT)
    right = split2(jnp.concatenate([meas, jnp.broadcast_to(cond_row * br_ref[...], (8, BALANCE))], axis=1))
    rcat = jnp.concatenate([right[0], right[1], right[0]], axis=1)
    for j in range(8):
        cols = slice(128 * j, 128 * j + 128)
        ids = 128 * j + lax.broadcasted_iota(jnp.int32, (128, SENSORS), 0)
        h = jnp.zeros((128, SENSORS), F32)
        for k in range(4):
            h = h + jnp.where(ids == st_ref[k : k + 1, :], co_ref[k : k + 1, :], 0.0)
        hh, hl = split2(h)
        hj = jnp.concatenate([hh, hh, hl], axis=1)
        hcat[cols, :] = hj
        s = dot(wcat[...], hj, NT)
        bids = 128 * j + lax.broadcasted_iota(jnp.int32, (BALANCE, 128), 1)
        bal = jnp.where(bids == ends[0], cond, 0.0) - jnp.where(bids == ends[1], cond, 0.0)
        fh, fl = split2(jnp.concatenate([s, bal], axis=0))
        sr[0:512, cols] = fh
        sr[512:1024, cols] = fh
        sr[1024:1536, cols] = fl
        prior = pr_ref[:, cols]
        ph, pm, pl_ = [part.astype(F32) for part in split3(prior)]
        none = jnp.zeros((80, 128), F32)
        sr[1536:1664, cols] = jnp.concatenate([ph, pm, ph, pl_, ph, pm, none], axis=0).astype(BF16)
        prt[cols, :] = jnp.transpose(jnp.concatenate([ph, ph, pm, ph, pl_, pm, none], axis=0)).astype(BF16)
        mom = dot(rcat, sr[0:1536, cols])[0:1, :] + jnp.sum(prior * info, axis=0, keepdims=True)
        for a in range(4):
            p0[a, 36, j : j + 1, :] = mom


def build_gram(core, half, en_ref, cd_ref, wcat, hcat, sr, prt, out):
    at = [pl.ds(pl.multiple_of(128 * i + 64 * core + 32 * half, 32), 32) for i in range(8)]
    st = dot(jnp.concatenate([hcat[r, :] for r in at], axis=0), wcat[...], NT)
    ids = lax.broadcasted_iota(jnp.int32, (32, BALANCE), 0) + (64 * core + 32 * half)
    cond = cd_ref[...]
    bal = [
        jnp.where(ids + 128 * i == en_ref[0:1, :], cond, 0.0) - jnp.where(ids + 128 * i == en_ref[1:2, :], cond, 0.0)
        for i in range(8)
    ]
    th, tl = split2(jnp.concatenate([st, jnp.concatenate(bal, axis=0)], axis=1))
    lhs = jnp.concatenate([th, tl, th, jnp.concatenate([prt[r, :] for r in at], axis=0)], axis=1)
    for j0 in range(0, 8, 2):
        wide = dot(lhs[0 : 32 * (j0 + 2), :], sr[:, 128 * j0 : 128 * j0 + 256])
        for j in (j0, j0 + 1):
            for i in range(j + 1):
                blk = wide[32 * i : 32 * i + 32, 128 * (j - j0) : 128 * (j - j0) + 128]
                out[:, FIRST[i] + j - i] = blk.reshape(4, 8, 128)


def lane_bc(x, lane):
    return jnp.broadcast_to(x[:, lane : lane + 1], (8, 128))


def row_bc(x, row):
    return jnp.broadcast_to(x[row : row + 1, :], (8, 128))


def factor_block(ds, rd, lt):
    lane = lax.broadcasted_iota(jnp.int32, (8, 128), 1)
    sub = lax.broadcasted_iota(jnp.int32, (8, 128), 0)
    t = [ds[8 * j : 8 * j + 8, :] for j in range(16)]
    c = [lane_bc(t[0], q) for q in range(8)]
    for g in range(16):
        r0 = 8 * g
        own = (lane >= r0) & (lane < r0 + 8)
        below = range(g + 1, 16)
        b = {j: [lane_bc(t[j], r0 + q) for q in range(8)] for j in below}
        if g < 15:
            nc = [lane_bc(t[g + 1], r0 + 8 + q) for q in range(8)]
        p = jnp.where(own, jnp.where(lane - r0 == sub, 1.0, 0.0), t[g])
        for j in below:
            t[j] = jnp.where(own, 0.0, t[j])
        w = []
        low = jnp.zeros((8, 128), F32)
        for s in range(8):
            inv = lax.rsqrt(row_bc(c[s], s))
            col = c[s] * inv
            mult = {q: row_bc(col, q) for q in range(s + 1, 8)}
            for q in range(s + 1, 8):
                c[q] = c[q] - col * mult[q]
            ws = row_bc(p, s) * inv
            if s < 7:
                p = p - col * ws
            low = jnp.where(lane == r0 + s, col, low)
            for j in below:
                m = b[j][s] * inv
                for q in range(s + 1, 8):
                    b[j][q] = b[j][q] - m * mult[q]
                t[j] = t[j] - m * ws
                if j == g + 1:
                    for q in range(8):
                        nc[q] = nc[q] - m * row_bc(m, q)
            w.append(ws)
        full = w[0]
        for s in range(1, 8):
            full = jnp.where(sub == s, w[s], full)
        rd[r0 : r0 + 8, :] = jnp.where(lane >= r0 + 8, full, 0.0)
        ds[r0 : r0 + 8, :] = jnp.where(lane < r0 + 8, full, 0.0)
        lt[r0 : r0 + 8, :] = low
        if g < 15:
            c = nc
    rd[...] = rd[...] + jnp.transpose(lt[...])


N_COPIES = 60


def kernel(
    w_in, st_in, co_in, rd_in, en_in, cd_in, br_in, pr_in, pi_in, t_in, r_ref, z_ref, x_ref,
    w_ref, st_ref, co_ref, rd_ref, en_ref, cd_ref, br_ref, pr_ref, pi_ref, t_s,
    wcat, hcat, sr, prt, p0, p1, r1a, r1b, q0, q1, r2a, r2b, zs, r3, b4, g,
    a_s, ds, rd, lt, di_s, rp_s, zv, in_sem, s_sem, r_sem,
):
    row = lax.axis_index("rows")
    core = lax.axis_index("cols")
    x, y, z = row // (NY * NZ), (row // NZ) % NY, row % NZ

    pairs = [
        (st_in, st_ref), (co_in, co_ref), (en_in, en_ref), (cd_in, cd_ref), (br_in, br_ref),
        (pr_in, pr_ref), (pi_in, pi_ref), (rd_in, rd_ref), (w_in, w_ref), (t_in, t_s),
    ]
    loads = [pltpu.make_async_copy(src, dst, in_sem.at[n]) for n, (src, dst) in enumerate(pairs)]
    for cp in loads:
        cp.start()

    def at_x(v, c=core):
        return ((v * NY + y) * NZ + z, c)

    def at_y(v, c=core):
        return ((x * NY + v) * NZ + z, c)

    def at_z(v):
        return ((x * NY + y) * NZ + v, core)

    other = 1 - core
    sibling = (row, other)
    hop = lambda v, d, n: lax.rem(v + d, n)
    xs = [hop(x, d, NX) for d in range(1, 4)]
    ys = [hop(y, d, NY) for d in range(1, 4)]
    zz = [hop(z, d, NZ) for d in range(1, 8)]
    barrier = pltpu.get_barrier_semaphore()
    friends = [at_x(v) for v in xs] + [at_y(v) for v in ys] + [at_z(v) for v in zz] + [sibling]
    friends += [at_x(v, other) for v in xs] + [at_y(v, other) for v in ys]
    for to in friends:
        pl.semaphore_signal(barrier, inc=1, device_id=to, device_id_type=MESH)

    copies = []

    def send(src, dst, to):
        n = len(copies)
        cp = pltpu.make_async_remote_copy(
            src_ref=src, dst_ref=dst, send_sem=s_sem.at[n], recv_sem=r_sem.at[n], device_id=to, device_id_type=MESH
        )
        cp.start()
        copies.append(cp)
        return cp

    for cp in loads[:-1]:
        cp.wait()
    build_rows(w_ref, st_ref, co_ref, rd_ref, en_ref, cd_ref, br_ref, pr_ref, pi_ref, wcat, hcat, sr, prt, p0, p1)
    build_gram(core, 0, en_ref, cd_ref, wcat, hcat, sr, prt, p0)
    pl.semaphore_wait(barrier, len(friends))
    wa = [send(p0.at[v], r1a.at[x], at_x(v)) for v in xs]
    build_gram(core, 1, en_ref, cd_ref, wcat, hcat, sr, prt, p1)
    wb = [send(p1.at[v], r1b.at[y], at_y(v)) for v in ys]
    r1a[x] = p0[x]
    r1b[y] = p1[y]
    for i in range(1, 8):
        a_s[i, :, :, 0:1024] = jnp.zeros((16, 8, 1024), F32)
    for cp in wa:
        cp.wait_recv()
    for b in range(4):
        t = slice(9 * b, 9 * b + 9)
        q0[b, 0:9] = (r1a[0, t] + r1a[1, t]) + (r1a[2, t] + r1a[3, t])
    m = (r1a[0, 36] + r1a[1, 36]) + (r1a[2, 36] + r1a[3, 36])
    for b in range(4):
        q0[b, 9] = m
    wa = [send(q0.at[v], r2a.at[y], at_y(v)) for v in ys]
    for cp in wb:
        cp.wait_recv()
    for b in range(4):
        t = slice(9 * b, 9 * b + 9)
        q1[b] = (r1b[0, t] + r1b[1, t]) + (r1b[2, t] + r1b[3, t])
    wb = [send(q1.at[v], r2b.at[x], at_x(v)) for v in xs]
    r2a[y] = q0[y]
    r2b[x] = q1[x]
    for cp in wa:
        cp.wait_recv()
    a0 = (r2a[0] + r2a[1]) + (r2a[2] + r2a[3])
    for cp in wb:
        cp.wait_recv()
    a1 = (r2b[0] + r2b[1]) + (r2b[2] + r2b[3])
    for n in range(3):
        zs[n, 0:3] = a0[3 * n : 3 * n + 3]
        zs[3 + n, 0:3] = a1[3 * n : 3 * n + 3]
    for n in range(2):
        zs[6 + n, 0:3] = jnp.zeros((3, 8, 128), F32)
    for n in range(8):
        zs[n, 3] = a0[9]
    wz = [send(zs.at[v], r3.at[z], at_z(v)) for v in zz]
    r3[z] = zs[z]
    for cp in wz:
        cp.wait_recv()
    total = ((r3[0] + r3[1]) + (r3[2] + r3[3])) + ((r3[4] + r3[5]) + (r3[6] + r3[7]))
    b4[z] = total[0:3]
    wz = [send(b4.at[z], b4.at[z], at_z(v)) for v in zz]
    moment = total[3]
    for i in range(8):
        a_s[i, :, :, 1024:] = spread(moment[i : i + 1, :]).reshape(16, 8, 128)
    for cp in wz:
        cp.wait_recv()
    for n in range(3):
        g[core, 0, x, pl.ds(9 * y + 3 * n, 3)] = b4[n]
        g[core, 1, y, pl.ds(9 * x + 3 * n, 3)] = b4[3 + n]
    mine = g.at[core, 0, x, pl.ds(9 * y, 9)]
    wa = [send(mine, mine, at_y(v)) for v in ys]
    mine = g.at[core, 1, y, pl.ds(9 * x, 9)]
    wb = [send(mine, mine, at_x(v)) for v in xs]
    HEAD, REST = pl.ds(0, 8), pl.ds(8, 28)
    for cp in wa:
        cp.wait_recv()
    mine = g.at[core, 0, x, HEAD]
    first = [send(mine, mine, to) for to in [at_x(v) for v in xs] + [at_x(v, other) for v in xs] + [sibling]]
    for cp in wb:
        cp.wait_recv()
    mine = g.at[core, 1, y, HEAD]
    first += [send(mine, mine, to) for to in [at_y(v) for v in ys] + [at_y(v, other) for v in ys] + [sibling]]
    mine = g.at[core, 0, x, REST]
    wa = [send(mine, mine, at_x(v)) for v in xs]
    last = [send(mine, mine, sibling)]
    mine = g.at[core, 1, y, REST]
    wb = [send(mine, mine, at_y(v)) for v in ys]
    last.append(send(mine, mine, sibling))
    for cp in first:
        cp.wait_recv()
    for j in range(8):
        for c in range(2):
            for h in range(2):
                a_s[0, 8 * c + 4 * h : 8 * c + 4 * h + 4, :, 128 * j : 128 * j + 128] = g[c, h, :, j]

    def relay(d, half):
        src = hop(x, NX - 1 - d, NX) if half == 0 else hop(y, NY - 1 - d, NY)
        got = g.at[core, half, src, pl.ds(8, 28)]
        n = N_COPIES - 6 + 2 * d + half
        return pltpu.make_async_remote_copy(
            src_ref=got, dst_ref=got, send_sem=s_sem.at[n], recv_sem=r_sem.at[n], device_id=sibling, device_id_type=MESH
        )

    def pass_on():
        for d in range(3):
            wa[d].wait_recv()
            relay(d, 0).start()
            wb[d].wait_recv()
            relay(d, 1).start()

    def take_rest():
        for cp in last:
            cp.wait_recv()
        for d in range(3):
            relay(d, 0).wait_recv()
            relay(d, 1).wait_recv()
        for i in range(1, 8):
            for j in range(i, 8):
                cols = slice(128 * j, 128 * j + 128)
                for c in range(2):
                    for h in range(2):
                        at = slice(8 * c + 4 * h, 8 * c + 4 * h + 4)
                        a_s[i, at, :, cols] = a_s[i, at, :, cols] + g[c, h, :, FIRST[i] + j - i]

    def block(i, j):
        at = slice(128 * j, 128 * j + 128) if isinstance(j, int) else pl.ds(pl.multiple_of(j * 128, 128), 128)
        return a_s[i, :, :, at].reshape(128, 128)

    def panel(k, _):
        @pl.when(k == 1)
        def _():
            take_rest()

        here = pl.ds(pl.multiple_of(k * 128, 128), 128)
        ds[...] = block(k, k)
        factor_block(ds, rd, lt)

        @pl.when(k == 0)
        def _():
            pass_on()

        di = ds[...]
        di_s[k] = di
        dh, dl = split2(di)
        dcat = jnp.concatenate([dh, dl, dh], axis=1)

        def columns(first):
            cols = slice(128 * first, 1152)
            ah, al = split2(a_s[k, :, :, cols].reshape(128, -1))
            r = dot(dcat, jnp.concatenate([ah, ah, al], axis=0))
            a_s[k, :, :, cols] = r.reshape(16, 8, -1)
            rh, rl = split2(r)
            rp_s[0:128, cols] = rh
            rp_s[128:256, cols] = rh
            rp_s[256:384, cols] = rl

        @pl.when(k < 4)
        def _():
            columns(1)

        @pl.when(k >= 4)
        def _():
            columns(5)

        a_s[k, :, :, here] = rd[...].reshape(16, 8, 128)

        for i in range(1, 8):

            @pl.when(i > k)
            def _():
                cols = slice(128 * i, 1152)
                th, tl = split2(jnp.transpose(block(k, i)))
                lhs = jnp.concatenate([th, tl, th], axis=1)
                a_s[i, :, :, cols] = a_s[i, :, :, cols] - dot(lhs, rp_s[:, cols]).reshape(16, 8, -1)

        return 0

    lax.fori_loop(0, 8, panel, 0)

    v = [jnp.transpose(block(i, 8))[0:8, :] for i in range(8)]
    for i in range(8):
        zv[i : i + 1, :] = v[i][0:1, :]
    z_ref[...] = zv[pl.ds(core * 4, 4), :]
    e = [None] * 8
    for k in range(7, -1, -1):
        e[k] = dot3(split2(v[k]), split2(di_s[k]))
        if k:
            above = a_s[0:k, :, :, 128 * k : 128 * k + 128].reshape(128 * k, 128)
            upd = dot3(split2(e[k]), split2(above), NT)
            for p in range(k):
                v[p] = v[p] - upd[:, 128 * p : 128 * p + 128]
    loads[-1].wait()
    nxt = dot3(split2(jnp.concatenate(e, axis=1)), split2(t_s[...]), NT)
    x_ref[...] = nxt[0:1, :]
    mine = a_s[row // 16, row % 16, :, pl.ds(pl.multiple_of(core * 512, 512), 512)]
    at_row = row * 8 + lax.broadcasted_iota(jnp.int32, (8, 512), 0)
    at_col = core * 512 + lax.broadcasted_iota(jnp.int32, (8, 512), 1)
    r_ref[...] = jnp.where(at_col >= at_row, mine, 0.0)
    for cp in copies:
        cp.wait_send()
    for d in range(3):
        relay(d, 0).wait_send()
        relay(d, 1).wait_send()


def per_device(
    whitening,
    sensor_states,
    sensor_coefficients,
    sensor_readings,
    conduit_endpoints,
    conductance,
    balance_right_side,
    prior_root_factor,
    prior_information,
    transition,
):
    args = (
        whitening,
        sensor_states.T,
        sensor_coefficients.T,
        sensor_readings.reshape(3, 128),
        conduit_endpoints.T,
        conductance.reshape(1, BALANCE),
        balance_right_side.reshape(1, BALANCE),
        prior_root_factor,
        prior_information.reshape(1, 8),
        transition,
    )
    vmem = pl.BlockSpec(memory_space=pltpu.VMEM)
    tiles = lambda *lead: pltpu.VMEM(lead + (8, 128), F32)
    r_post, z_post, x_next = pl.pallas_call(
        kernel,
        out_shape=(
            jax.ShapeDtypeStruct((8, 512), F32),
            jax.ShapeDtypeStruct((4, 128), F32),
            jax.ShapeDtypeStruct((1, 512), F32),
        ),
        in_specs=[pl.BlockSpec(memory_space=pl.ANY)] * len(args),
        out_specs=(vmem, vmem, vmem),
        scratch_shapes=[pltpu.VMEM(arg.shape, arg.dtype) for arg in args]
        + [
            pltpu.VMEM((SENSORS, 3 * SENSORS), BF16),
            pltpu.VMEM((1024, 3 * SENSORS), BF16),
            pltpu.VMEM((DEPTH, 1024), BF16),
            pltpu.VMEM((1024, 128), BF16),
            tiles(4, 37),
            tiles(4, 36),
            tiles(4, 37),
            tiles(4, 36),
            tiles(4, 10),
            tiles(4, 9),
            tiles(4, 10),
            tiles(4, 9),
            tiles(8, 4),
            tiles(8, 4),
            tiles(8, 3),
            tiles(2, 2, 4, 36),
            pltpu.VMEM((8, 16, 8, 1152), F32),
            pltpu.VMEM((128, 128), F32),
            pltpu.VMEM((128, 128), F32),
            pltpu.VMEM((128, 128), F32),
            pltpu.VMEM((8, 128, 128), F32),
            pltpu.VMEM((384, 1152), BF16),
            pltpu.VMEM((8, 128), F32),
            pltpu.SemaphoreType.DMA((10,)),
            pltpu.SemaphoreType.DMA((N_COPIES,)),
            pltpu.SemaphoreType.DMA((N_COPIES,)),
        ],
        compiler_params=pltpu.CompilerParams(
            collective_id=0, has_side_effects=True, vmem_limit_bytes=62 * 1024 * 1024
        ),
    )(*args)
    return r_post, z_post.reshape(512), x_next.reshape(512)


def solution(mesh):
    in_specs = (
        P("rows", None),
        P("rows", None),
        P("rows", None),
        P("rows"),
        P("rows", None),
        P("rows"),
        P("rows"),
        P("rows", None),
        P("rows"),
        P("cols", None),
    )
    out_specs = (P("rows", "cols"), P("cols"), P("cols"))
    return jax.shard_map(
        per_device, mesh=mesh, in_specs=in_specs, out_specs=out_specs, check_vma=False
    )
```

time: 972 us -> 93.9 us (0.10)
  the two profiles are of different devices: /device:TPU:0 before, /device:TPU:1 now
where the time goes in v3:
time: 93.9 us; the launch traced here: 93.6 us
  Pallas kernels  89.1 us (95%)
  local copies, waits for them, and re-layouts  3.8 us (4%)
    pallas_call x1, Pallas kernels, per_device(): pl.pallas_call(kernel, out_shape=(jax.ShapeDtypeStruct((8, 512), F32), ja...  89.1 us
    unnamed x3, local copies, waits for them, and re-layouts  3.8 us

profile of v3, /device:TPU:1, one launch (start us, length us, event | category | flops | bytes accessed | tf_op | source)
XLA Modules:
  0.0 93.6 jit_solution(18293778902663497402)
XLA Ops:
  0.6 89.1 %shard_map.121 = (f32[8,512]{1,0:T(8,128)}, f32[4,128]{1,0:T(4,128)}, f32[1,512]{1,0:T(1,128)}) custom-call(f32[384,384]{1,0:T(8,128)} %w_in.1, s32[4,384]{1,0:T(4,128)} %bitcast.9, f32[4,384]{1,0:T(4,128)} %bitcast.10, f32[3,128]{1,0:T(4,128)} %bitcast.13, s32[2,128]{1,0:T(2,128)} %bitcast.14, f32[1,128]{1,0:T(1,128)} %bitcast.15, f32[1,128]{1,0:T(1,128)} %bitcast.16, ...), custom_call_target="tpu_custom_call" | custom-call | tf_op jit(solution)/shard_map/pallas_call | solution.py:426
  89.8 1.3 %copy.16 = f32[8,512]{1,0:T(8,128)} copy(f32[8,512]{1,0:T(8,128)} %get-tuple-element.12) | data formatting | bytes 32768
  91.1 1.2 %copy.17 = f32[512]{0:T(512)} copy(f32[512]{0:T(512)} %bitcast.12) | data formatting | bytes 4096
  92.3 1.2 %copy.18 = f32[512]{0:T(512)} copy(f32[512]{0:T(512)} %bitcast.11) | data formatting | bytes 4096

commit v4 on v3

--- a/solution.py
+++ b/solution.py
@@ -104,7 +104,10 @@
     return jnp.broadcast_to(x[row : row + 1, :], (8, 128))
 
 
-def factor_block(ds, rd, lt):
+NEAR = 8
+
+
+def factor_block(ds, rd, lt, beside):
     lane = lax.broadcasted_iota(jnp.int32, (8, 128), 1)
     sub = lax.broadcasted_iota(jnp.int32, (8, 128), 0)
     t = [ds[8 * j : 8 * j + 8, :] for j in range(16)]
@@ -112,14 +115,16 @@
     for g in range(16):
         r0 = 8 * g
         own = (lane >= r0) & (lane < r0 + 8)
-        below = range(g + 1, 16)
-        b = {j: [lane_bc(t[j], r0 + q) for q in range(8)] for j in below}
+        near = range(g + 1, min(16, g + 1 + NEAR))
+        far = range(g + 1 + NEAR, 16)
+        b = {j: [lane_bc(t[j], r0 + q) for q in range(8)] for j in near}
         if g < 15:
             nc = [lane_bc(t[g + 1], r0 + 8 + q) for q in range(8)]
         p = jnp.where(own, jnp.where(lane - r0 == sub, 1.0, 0.0), t[g])
-        for j in below:
+        raw = split2(jnp.concatenate([t[j] for j in far], axis=0)) if far else None
+        for j in range(g + 1, 16):
             t[j] = jnp.where(own, 0.0, t[j])
-        w = []
+        w, mults, invs = [], [], []
         low = jnp.zeros((8, 128), F32)
         for s in range(8):
             inv = lax.rsqrt(row_bc(c[s], s))
@@ -131,7 +136,7 @@
             if s < 7:
                 p = p - col * ws
             low = jnp.where(lane == r0 + s, col, low)
-            for j in below:
+            for j in near:
                 m = b[j][s] * inv
                 for q in range(s + 1, 8):
                     b[j][q] = b[j][q] - m * mult[q]
@@ -140,14 +145,36 @@
                     for q in range(8):
                         nc[q] = nc[q] - m * row_bc(m, q)
             w.append(ws)
+            mults.append(mult)
+            invs.append(inv)
         full = w[0]
         for s in range(1, 8):
             full = jnp.where(sub == s, w[s], full)
+        if far:
+            y = [None] * 8
+            for s in range(7, -1, -1):
+                v = w[s]
+                for q in range(7, s, -1):
+                    v = v - mults[s][q] * y[q]
+                y[s] = v * invs[s]
+            yy = y[0]
+            for s in range(1, 8):
+                yy = jnp.where(sub == s, y[s], yy)
+            pad = lambda v: jnp.concatenate(
+                ([jnp.zeros((r0, 128), F32)] if r0 else []) + [v, jnp.zeros((120 - r0, 128), F32)], axis=0
+            ).astype(BF16)
+            yh = yy.astype(BF16).astype(F32)
+            yhp, ylp = pad(yh), pad(yy - yh)
+            upd = dot(jnp.concatenate(raw, axis=1), jnp.concatenate([yhp, yhp], axis=0)) + dot(raw[0], ylp)
+            for n, j in enumerate(far):
+                t[j] = t[j] - upd[8 * n : 8 * n + 8, :]
         rd[r0 : r0 + 8, :] = jnp.where(lane >= r0 + 8, full, 0.0)
         ds[r0 : r0 + 8, :] = jnp.where(lane < r0 + 8, full, 0.0)
         lt[r0 : r0 + 8, :] = low
         if g < 15:
             c = nc
+        for step in beside[g]:
+            step()
     rd[...] = rd[...] + jnp.transpose(lt[...])
 
 
@@ -155,10 +182,10 @@
 
 
 def kernel(
-    w_in, st_in, co_in, rd_in, en_in, cd_in, br_in, pr_in, pi_in, t_in, r_ref, z_ref, x_ref,
+    w_in, st_in, co_in, rd_in, en_in, cd_in, br_in, pr_in, pi_in, t_in, o_ref,
     w_ref, st_ref, co_ref, rd_ref, en_ref, cd_ref, br_ref, pr_ref, pi_ref, t_s,
     wcat, hcat, sr, prt, p0, p1, r1a, r1b, q0, q1, r2a, r2b, zs, r3, b4, g,
-    a_s, ds, rd, lt, di_s, rp_s, zv, in_sem, s_sem, r_sem,
+    a_s, ds, rd, lt, dh_s, dl_s, rp_s, rt_s, rh_s, rl_s, th_s, tl_s, zv, in_sem, s_sem, r_sem,
 ):
     row = lax.axis_index("rows")
     core = lax.axis_index("cols")
@@ -216,6 +243,11 @@
     r1b[y] = p1[y]
     for i in range(1, 8):
         a_s[i, :, :, 0:1024] = jnp.zeros((16, 8, 1024), F32)
+    a_s[8] = jnp.zeros((16, 8, 1152), F32)
+    dh_s[8] = jnp.zeros((128, 128), BF16)
+    dl_s[8] = jnp.zeros((128, 128), BF16)
+    loads[-1].wait()
+    th_s[...], tl_s[...] = split2(t_s[...])
     for cp in wa:
         cp.wait_recv()
     for b in range(4):
@@ -316,85 +348,97 @@
                         at = slice(8 * c + 4 * h, 8 * c + 4 * h + 4)
                         a_s[i, at, :, cols] = a_s[i, at, :, cols] + g[c, h, :, FIRST[i] + j - i]
 
-    def block(i, j):
-        at = slice(128 * j, 128 * j + 128) if isinstance(j, int) else pl.ds(pl.multiple_of(j * 128, 128), 128)
-        return a_s[i, :, :, at].reshape(128, 128)
-
     def panel(k, _):
         @pl.when(k == 1)
         def _():
             take_rest()
-
-        here = pl.ds(pl.multiple_of(k * 128, 128), 128)
-        ds[...] = block(k, k)
-        factor_block(ds, rd, lt)
+            for c in range(2):
+                for h in range(2):
+                    at = slice(64 * c + 32 * h, 64 * c + 32 * h + 32)
+                    ds[at, :] = ds[at, :] + g[c, h, :, FIRST[1]].reshape(32, 128)
+
+        prev = jnp.where(k == 0, 8, k - 1)
+        dcat = jnp.concatenate([dh_s[prev], dl_s[prev], dh_s[prev]], axis=1)
+
+        def product(j):
+            def step():
+                cols = slice(128 * j, 128 * j + 256)
+                ah, al = split2(a_s[prev, :, :, cols].reshape(128, 256))
+                r = dot(dcat, jnp.concatenate([ah, ah, al], axis=0))
+                a_s[prev, :, :, cols] = r.reshape(16, 8, 256)
+                rh, rl = split2(r)
+                rp_s[0:128, cols] = rh
+                rp_s[128:256, cols] = rh
+                rp_s[256:384, cols] = rl
+                rh_s[prev, :, cols] = rh
+                rl_s[prev, :, cols] = rl
+                for i in range(j, min(j + 2, 8)):
+                    th, tl = split2(jnp.transpose(r[:, 128 * (i - j) : 128 * (i - j) + 128]))
+                    rt_s[i] = jnp.concatenate([th, tl, th], axis=1)
+
+            return step
+
+        def update(i, j):
+            def step():
+                end = min(j + 2, 9)
+                cols = slice(128 * j, 128 * end)
+                to = jnp.where(i >= k, i, 8)
+                upd = dot(rt_s[i], rp_s[:, cols])
+                a_s[to, :, :, cols] = a_s[to, :, :, cols] - upd.reshape(16, 8, 128 * (end - j))
+
+            return step
+
+        steps = [product(j) for j in range(1, 9, 2)]
+        steps += [update(i, j) for i in range(1, 8) for j in range(i, 9, 2)]
+        factor_block(ds, rd.at[k], lt, [steps[2 * n : 2 * n + 2] for n in range(16)])
 
         @pl.when(k == 0)
         def _():
             pass_on()
 
-        di = ds[...]
-        di_s[k] = di
-        dh, dl = split2(di)
-        dcat = jnp.concatenate([dh, dl, dh], axis=1)
-
-        def columns(first):
-            cols = slice(128 * first, 1152)
-            ah, al = split2(a_s[k, :, :, cols].reshape(128, -1))
-            r = dot(dcat, jnp.concatenate([ah, ah, al], axis=0))
-            a_s[k, :, :, cols] = r.reshape(16, 8, -1)
-            rh, rl = split2(r)
-            rp_s[0:128, cols] = rh
-            rp_s[128:256, cols] = rh
-            rp_s[256:384, cols] = rl
-
-        @pl.when(k < 4)
-        def _():
-            columns(1)
-
-        @pl.when(k >= 4)
-        def _():
-            columns(5)
-
-        a_s[k, :, :, here] = rd[...].reshape(16, 8, 128)
-
-        for i in range(1, 8):
-
-            @pl.when(i > k)
-            def _():
-                cols = slice(128 * i, 1152)
-                th, tl = split2(jnp.transpose(block(k, i)))
-                lhs = jnp.concatenate([th, tl, th], axis=1)
-                a_s[i, :, :, cols] = a_s[i, :, :, cols] - dot(lhs, rp_s[:, cols]).reshape(16, 8, -1)
-
+        d = split2(ds[...])
+        dh_s[k], dl_s[k] = d
+        nxt = pl.ds(pl.multiple_of(128 * k + 128, 128), 128)
+        c = dot3(d, split2(a_s[k, :, :, nxt].reshape(128, 128)))
+        ds[...] = a_s[k + 1, :, :, nxt].reshape(128, 128) - dot3(split2(jnp.transpose(c)), split2(c))
         return 0
 
+    ds[...] = a_s[0, :, :, 0:128].reshape(128, 128)
     lax.fori_loop(0, 8, panel, 0)
 
-    v = [jnp.transpose(block(i, 8))[0:8, :] for i in range(8)]
+    z7 = dot3((dh_s[7], dl_s[7]), split2(a_s[7, :, :, 1024:].reshape(128, 128)))
+    v = [jnp.transpose(a_s[i, :, :, 1024:].reshape(128, 128))[0:8, :] for i in range(7)] + [jnp.transpose(z7)[0:8, :]]
     for i in range(8):
         zv[i : i + 1, :] = v[i][0:1, :]
-    z_ref[...] = zv[pl.ds(core * 4, 4), :]
     e = [None] * 8
     for k in range(7, -1, -1):
-        e[k] = dot3(split2(v[k]), split2(di_s[k]))
-        if k:
-            above = a_s[0:k, :, :, 128 * k : 128 * k + 128].reshape(128 * k, 128)
-            upd = dot3(split2(e[k]), split2(above), NT)
-            for p in range(k):
-                v[p] = v[p] - upd[:, 128 * p : 128 * p + 128]
-    loads[-1].wait()
-    nxt = dot3(split2(jnp.concatenate(e, axis=1)), split2(t_s[...]), NT)
-    x_ref[...] = nxt[0:1, :]
+        e[k] = dot3(split2(v[k]), (dh_s[k], dl_s[k]))
+        ek = split2(e[k])
+        for p in range(k - 1, -1, -1):
+            at = slice(128 * k, 128 * k + 128)
+            v[p] = v[p] - dot3(ek, (rh_s[p, :, at], rl_s[p, :, at]), NT)
+    nxt = dot3(split2(jnp.concatenate(e, axis=1)), (th_s[...], tl_s[...]), NT)
+    for q in range(4):
+        o_ref[8:9, 128 * q : 128 * q + 128] = zv[pl.ds(core * 4 + q, 1), :]
+    o_ref[9:10, :] = nxt[0:1, :]
+    o_ref[10:16, :] = jnp.zeros((6, 512), F32)
+    for k in range(8):
+        a_s[k, :, :, 128 * k : 128 * k + 128] = rd[k].reshape(16, 8, 128)
     mine = a_s[row // 16, row % 16, :, pl.ds(pl.multiple_of(core * 512, 512), 512)]
     at_row = row * 8 + lax.broadcasted_iota(jnp.int32, (8, 512), 0)
     at_col = core * 512 + lax.broadcasted_iota(jnp.int32, (8, 512), 1)
-    r_ref[...] = jnp.where(at_col >= at_row, mine, 0.0)
+    o_ref[0:8, :] = jnp.where(at_col >= at_row, mine, 0.0)
     for cp in copies:
         cp.wait_send()
     for d in range(3):
         relay(d, 0).wait_send()
         relay(d, 1).wait_send()
+
+
+def hand_out(all_ref, r_ref, z_ref, x_ref):
+    r_ref[...] = all_ref[0:8, :]
+    z_ref[...] = all_ref[8:9, :]
+    x_ref[...] = all_ref[9:10, :]
 
 
 def per_device(
@@ -423,15 +467,11 @@
     )
     vmem = pl.BlockSpec(memory_space=pltpu.VMEM)
     tiles = lambda *lead: pltpu.VMEM(lead + (8, 128), F32)
-    r_post, z_post, x_next = pl.pallas_call(
+    results = pl.pallas_call(
         kernel,
-        out_shape=(
-            jax.ShapeDtypeStruct((8, 512), F32),
-            jax.ShapeDtypeStruct((4, 128), F32),
-            jax.ShapeDtypeStruct((1, 512), F32),
-        ),
+        out_shape=jax.ShapeDtypeStruct((16, 512), F32),
         in_specs=[pl.BlockSpec(memory_space=pl.ANY)] * len(args),
-        out_specs=(vmem, vmem, vmem),
+        out_specs=vmem,
         scratch_shapes=[pltpu.VMEM(arg.shape, arg.dtype) for arg in args]
         + [
             pltpu.VMEM((SENSORS, 3 * SENSORS), BF16),
@@ -450,12 +490,18 @@
             tiles(8, 4),
             tiles(8, 3),
             tiles(2, 2, 4, 36),
-            pltpu.VMEM((8, 16, 8, 1152), F32),
-            pltpu.VMEM((128, 128), F32),
-            pltpu.VMEM((128, 128), F32),
+            pltpu.VMEM((9, 16, 8, 1152), F32),
             pltpu.VMEM((128, 128), F32),
             pltpu.VMEM((8, 128, 128), F32),
+            pltpu.VMEM((128, 128), F32),
+            pltpu.VMEM((9, 128, 128), BF16),
+            pltpu.VMEM((9, 128, 128), BF16),
             pltpu.VMEM((384, 1152), BF16),
+            pltpu.VMEM((8, 128, 384), BF16),
+            pltpu.VMEM((9, 128, 1152), BF16),
+            pltpu.VMEM((9, 128, 1152), BF16),
+            pltpu.VMEM((512, 1024), BF16),
+            pltpu.VMEM((512, 1024), BF16),
             pltpu.VMEM((8, 128), F32),
             pltpu.SemaphoreType.DMA((10,)),
             pltpu.SemaphoreType.DMA((N_COPIES,)),
@@ -465,6 +511,17 @@
             collective_id=0, has_side_effects=True, vmem_limit_bytes=62 * 1024 * 1024
         ),
     )(*args)
+    r_post, z_post, x_next = pl.pallas_call(
+        hand_out,
+        out_shape=(
+            jax.ShapeDtypeStruct((8, 512), F32),
+            jax.ShapeDtypeStruct((1, 512), F32),
+            jax.ShapeDtypeStruct((1, 512), F32),
+        ),
+        in_specs=[vmem],
+        out_specs=(vmem, vmem, vmem),
+        compiler_params=pltpu.CompilerParams(vmem_limit_bytes=62 * 1024 * 1024),
+    )(results)
     return r_post, z_post.reshape(512), x_next.reshape(512)
 
 

time: 93.9 us -> 86.7 us (0.923)
  local copies, waits for them, and re-layouts: 3.8 us -> 0 us
  Pallas kernels: 89.1 us -> 85.9 us
    unnamed x3 -> x0, local copies, waits for them, and re-layouts: 3.8 us -> none
    pallas_call x1 -> x2, Pallas kernels: 89.1 us -> 85.9 us  [the longest x1 84.5 us: per_device(): pl.pallas_call(kernel, out_shape=jax.ShapeDtypeStruct((16, 512), F32), in...]
where the time goes in v4:
time: 86.7 us; the launch traced here: 86.6 us
  Pallas kernels  85.9 us (99%)
    pallas_call x1, Pallas kernels, per_device(): pl.pallas_call(kernel, out_shape=jax.ShapeDtypeStruct((16, 512), F32), in...  84.5 us

profile of v4, /device:TPU:1, one launch (start us, length us, event | category | flops | bytes accessed | tf_op | source)
XLA Modules:
  0.0 86.6 jit_solution(2209619827096413582)
XLA Ops:
  0.6 84.5 %shard_map.121.all_ref = f32[16,512]{1,0:T(8,128)} custom-call(f32[384,384]{1,0:T(8,128)} %w_in.1, s32[4,384]{1,0:T(4,128)} %bitcast.9, f32[4,384]{1,0:T(4,128)} %bitcast.10, f32[3,128]{1,0:T(4,128)} %bitcast.11, s32[2,128]{1,0:T(2,128)} %bitcast.12, f32[1,128]{1,0:T(1,128)} %bitcast.13, f32[1,128]{1,0:T(1,128)} %bitcast.14, f32[8,1024]{1,0:T(8,128)} %pr_in.1, ...), custom_call_target="tpu_custom_call" | custom-call | tf_op jit(solution)/shard_map/pallas_call | solution.py:470
  85.2 1.4 %shard_map.122 = (f32[8,512]{1,0:T(8,128)}, f32[1,512]{1,0:T(1,128)}, f32[1,512]{1,0:T(1,128)}) custom-call(f32[16,512]{1,0:T(8,128)} %shard_map.121.all_ref), custom_call_target="tpu_custom_call" | custom-call | tf_op jit(solution)/shard_map/pallas_call | solution.py:514

commit v5 on v4

--- a/solution.py
+++ b/solution.py
@@ -11,6 +11,7 @@
 SENSORS, BALANCE = 384, 128
 DEPTH = 3 * (SENSORS + BALANCE) + 128
 FIRST = [0, 8, 15, 21, 26, 30, 33, 35, 36]
+HEAD, REST = 16, 20
 NN = (((1,), (0,)), ((), ()))
 NT = (((1,), (1,)), ((), ()))
 TN = (((0,), (0,)), ((), ()))
@@ -74,7 +75,7 @@
         prt[cols, :] = jnp.transpose(jnp.concatenate([ph, ph, pm, ph, pl_, pm, none], axis=0)).astype(BF16)
         mom = dot(rcat, sr[0:1536, cols])[0:1, :] + jnp.sum(prior * info, axis=0, keepdims=True)
         for a in range(4):
-            p0[a, 36, j : j + 1, :] = mom
+            p0[a, HEAD, j : j + 1, :] = mom
 
 
 def build_gram(core, half, en_ref, cd_ref, wcat, hcat, sr, prt, out):
@@ -93,7 +94,8 @@
         for j in (j0, j0 + 1):
             for i in range(j + 1):
                 blk = wide[32 * i : 32 * i + 32, 128 * (j - j0) : 128 * (j - j0) + 128]
-                out[:, FIRST[i] + j - i] = blk.reshape(4, 8, 128)
+                at = FIRST[i] + j - i
+                out[:, at + (1 if half == 0 and at >= HEAD else 0)] = blk.reshape(4, 8, 128)
 
 
 def lane_bc(x, lane):
@@ -178,13 +180,14 @@
     rd[...] = rd[...] + jnp.transpose(lt[...])
 
 
-N_COPIES = 60
+LATE = 86
+N_COPIES = LATE + 20
 
 
 def kernel(
     w_in, st_in, co_in, rd_in, en_in, cd_in, br_in, pr_in, pi_in, t_in, o_ref,
     w_ref, st_ref, co_ref, rd_ref, en_ref, cd_ref, br_ref, pr_ref, pi_ref, t_s,
-    wcat, hcat, sr, prt, p0, p1, r1a, r1b, q0, q1, r2a, r2b, zs, r3, b4, g,
+    wcat, hcat, sr, prt, p0, p1, r1, q, r2, zs, r3, b4, g,
     a_s, ds, rd, lt, dh_s, dl_s, rp_s, rt_s, rh_s, rl_s, th_s, tl_s, zv, in_sem, s_sem, r_sem,
 ):
     row = lax.axis_index("rows")
@@ -222,25 +225,94 @@
 
     copies = []
 
-    def send(src, dst, to):
-        n = len(copies)
-        cp = pltpu.make_async_remote_copy(
+    def remote(n, src, dst, to):
+        return pltpu.make_async_remote_copy(
             src_ref=src, dst_ref=dst, send_sem=s_sem.at[n], recv_sem=r_sem.at[n], device_id=to, device_id_type=MESH
         )
+
+    def send(src, dst, to):
+        cp = remote(len(copies), src, dst, to)
         cp.start()
         copies.append(cp)
         return cp
 
+    def arrive(these):
+        for cp in these:
+            cp.wait_recv()
+
     for cp in loads[:-1]:
         cp.wait()
     build_rows(w_ref, st_ref, co_ref, rd_ref, en_ref, cd_ref, br_ref, pr_ref, pi_ref, wcat, hcat, sr, prt, p0, p1)
+    me = [(x, y), (y, x)]
+    peers = [(xs, ys), (ys, xs)]
+    place = [(at_x, at_y), (at_y, at_x)]
+
+    def first_out(c, h):
+        p = (p0, p1)[h]
+        n = r1[c][h].shape[1]
+        start = c * (p.shape[1] - REST)
+        own = me[h][0]
+        out = [send(p.at[v, pl.ds(start, n)], r1[c][h].at[own], place[h][0](v)) for v in peers[h][0]]
+        r1[c][h][own] = p[own, start : start + n]
+        return out
+
+    def second_out(c, h):
+        size = (HEAD, REST)[c] // 4
+        got = r1[c][h]
+        for b in range(4):
+            t = slice(size * b, size * b + size)
+            q[c][h][b, 0:size] = (got[0, t] + got[1, t]) + (got[2, t] + got[3, t])
+            if c == 0 and h == 0:
+                q[c][h][b, size] = (got[0, HEAD] + got[1, HEAD]) + (got[2, HEAD] + got[3, HEAD])
+        own = me[h][1]
+        out = [send(q[c][h].at[v], r2[c][h].at[own], place[h][1](v)) for v in peers[h][1]]
+        r2[c][h][own] = q[c][h][own]
+        return out
+
+    def z_out(c):
+        a0, a1 = [(r2[c][h][0] + r2[c][h][1]) + (r2[c][h][2] + r2[c][h][3]) for h in range(2)]
+        if c == 0:
+            for n in range(4):
+                zs[0][n, 0] = a0[n]
+                zs[0][4 + n, 0] = a1[n]
+            for n in range(8):
+                zs[0][n, 1] = a0[4]
+        else:
+            for n in range(5):
+                zs[1][n // 2, n % 2] = a0[n]
+                zs[1][(5 + n) // 2, (5 + n) % 2] = a1[n]
+            for n in range(5, 8):
+                zs[1][n] = jnp.zeros((2, 8, 128), F32)
+        out = [send(zs[c].at[v], r3[c].at[z], at_z(v)) for v in zz]
+        r3[c][z] = zs[c][z]
+        return out
+
+    def z_back(c):
+        total = [r3[c][n] for n in range(8)]
+        total = ((total[0] + total[1]) + (total[2] + total[3])) + ((total[4] + total[5]) + (total[6] + total[7]))
+        size = 1 + c
+        b4[c][z] = total[0:size]
+        out = [send(b4[c].at[z], b4[c].at[z], at_z(v)) for v in zz]
+        return out, total[1]
+
+    def second_back(c):
+        size = (HEAD, REST)[c] // 4
+        out = []
+        for h in range(2):
+            begin = c * HEAD + size * me[h][1]
+            for n in range(size):
+                at = size * h + n
+                g[core, h, me[h][0], begin + n] = b4[c][at // (1 + c), at % (1 + c)]
+            mine = g.at[core, h, me[h][0], pl.ds(begin, size)]
+            out.append([send(mine, mine, place[h][1](v)) for v in peers[h][1]])
+        return out
+
     build_gram(core, 0, en_ref, cd_ref, wcat, hcat, sr, prt, p0)
     pl.semaphore_wait(barrier, len(friends))
-    wa = [send(p0.at[v], r1a.at[x], at_x(v)) for v in xs]
+    one0 = [first_out(0, 0)]
     build_gram(core, 1, en_ref, cd_ref, wcat, hcat, sr, prt, p1)
-    wb = [send(p1.at[v], r1b.at[y], at_y(v)) for v in ys]
-    r1a[x] = p0[x]
-    r1b[y] = p1[y]
+    one0.append(first_out(0, 1))
+    one1 = [first_out(1, 0), first_out(1, 1)]
     for i in range(1, 8):
         a_s[i, :, :, 0:1024] = jnp.zeros((16, 8, 1024), F32)
     a_s[8] = jnp.zeros((16, 8, 1152), F32)
@@ -248,114 +320,86 @@
     dl_s[8] = jnp.zeros((128, 128), BF16)
     loads[-1].wait()
     th_s[...], tl_s[...] = split2(t_s[...])
-    for cp in wa:
-        cp.wait_recv()
-    for b in range(4):
-        t = slice(9 * b, 9 * b + 9)
-        q0[b, 0:9] = (r1a[0, t] + r1a[1, t]) + (r1a[2, t] + r1a[3, t])
-    m = (r1a[0, 36] + r1a[1, 36]) + (r1a[2, 36] + r1a[3, 36])
-    for b in range(4):
-        q0[b, 9] = m
-    wa = [send(q0.at[v], r2a.at[y], at_y(v)) for v in ys]
-    for cp in wb:
-        cp.wait_recv()
-    for b in range(4):
-        t = slice(9 * b, 9 * b + 9)
-        q1[b] = (r1b[0, t] + r1b[1, t]) + (r1b[2, t] + r1b[3, t])
-    wb = [send(q1.at[v], r2b.at[x], at_x(v)) for v in xs]
-    r2a[y] = q0[y]
-    r2b[x] = q1[x]
-    for cp in wa:
-        cp.wait_recv()
-    a0 = (r2a[0] + r2a[1]) + (r2a[2] + r2a[3])
-    for cp in wb:
-        cp.wait_recv()
-    a1 = (r2b[0] + r2b[1]) + (r2b[2] + r2b[3])
-    for n in range(3):
-        zs[n, 0:3] = a0[3 * n : 3 * n + 3]
-        zs[3 + n, 0:3] = a1[3 * n : 3 * n + 3]
-    for n in range(2):
-        zs[6 + n, 0:3] = jnp.zeros((3, 8, 128), F32)
-    for n in range(8):
-        zs[n, 3] = a0[9]
-    wz = [send(zs.at[v], r3.at[z], at_z(v)) for v in zz]
-    r3[z] = zs[z]
-    for cp in wz:
-        cp.wait_recv()
-    total = ((r3[0] + r3[1]) + (r3[2] + r3[3])) + ((r3[4] + r3[5]) + (r3[6] + r3[7]))
-    b4[z] = total[0:3]
-    wz = [send(b4.at[z], b4.at[z], at_z(v)) for v in zz]
-    moment = total[3]
+    two0, two1 = [], []
+    for h in range(2):
+        arrive(one0[h])
+        two0.append(second_out(0, h))
+    for h in range(2):
+        arrive(one1[h])
+        two1.append(second_out(1, h))
+    arrive(two0[0] + two0[1])
+    z0 = z_out(0)
+    arrive(two1[0] + two1[1])
+    z1 = z_out(1)
+    arrive(z0)
+    back0, moment = z_back(0)
     for i in range(8):
         a_s[i, :, :, 1024:] = spread(moment[i : i + 1, :]).reshape(16, 8, 128)
-    for cp in wz:
-        cp.wait_recv()
-    for n in range(3):
-        g[core, 0, x, pl.ds(9 * y + 3 * n, 3)] = b4[n]
-        g[core, 1, y, pl.ds(9 * x + 3 * n, 3)] = b4[3 + n]
-    mine = g.at[core, 0, x, pl.ds(9 * y, 9)]
-    wa = [send(mine, mine, at_y(v)) for v in ys]
-    mine = g.at[core, 1, y, pl.ds(9 * x, 9)]
-    wb = [send(mine, mine, at_x(v)) for v in xs]
-    HEAD, REST = pl.ds(0, 8), pl.ds(8, 28)
-    for cp in wa:
-        cp.wait_recv()
-    mine = g.at[core, 0, x, HEAD]
-    first = [send(mine, mine, to) for to in [at_x(v) for v in xs] + [at_x(v, other) for v in xs] + [sibling]]
-    for cp in wb:
-        cp.wait_recv()
-    mine = g.at[core, 1, y, HEAD]
-    first += [send(mine, mine, to) for to in [at_y(v) for v in ys] + [at_y(v, other) for v in ys] + [sibling]]
-    mine = g.at[core, 0, x, REST]
-    wa = [send(mine, mine, at_x(v)) for v in xs]
-    last = [send(mine, mine, sibling)]
-    mine = g.at[core, 1, y, REST]
-    wb = [send(mine, mine, at_y(v)) for v in ys]
-    last.append(send(mine, mine, sibling))
-    for cp in first:
-        cp.wait_recv()
+    arrive(z1)
+    back1, _ = z_back(1)
+    arrive(back0)
+    two0 = second_back(0)
+    arrive(back1)
+    two1 = second_back(1)
+    top = []
+    for h in range(2):
+        arrive(two0[h])
+        mine = g.at[core, h, me[h][0], pl.ds(0, 8)]
+        for c in (core, other):
+            top += [send(mine, mine, place[h][0](v, c)) for v in peers[h][0]]
+        top.append(send(mine, mine, sibling))
+    row1, row1_own = [], []
+    for h in range(2):
+        mine = g.at[core, h, me[h][0], pl.ds(8, 8)]
+        row1.append([send(mine, mine, place[h][0](v)) for v in peers[h][0]])
+        row1_own.append(send(mine, mine, sibling))
+    assert len(copies) == LATE
+    arrive(top)
     for j in range(8):
         for c in range(2):
             for h in range(2):
                 a_s[0, 8 * c + 4 * h : 8 * c + 4 * h + 4, :, 128 * j : 128 * j + 128] = g[c, h, :, j]
 
-    def relay(d, half):
-        src = hop(x, NX - 1 - d, NX) if half == 0 else hop(y, NY - 1 - d, NY)
-        got = g.at[core, half, src, pl.ds(8, 28)]
-        n = N_COPIES - 6 + 2 * d + half
-        return pltpu.make_async_remote_copy(
-            src_ref=got, dst_ref=got, send_sem=s_sem.at[n], recv_sem=r_sem.at[n], device_id=sibling, device_id_type=MESH
-        )
-
-    def pass_on():
-        for d in range(3):
-            wa[d].wait_recv()
-            relay(d, 0).start()
-            wb[d].wait_recv()
-            relay(d, 1).start()
-
-    def take_rest():
-        for cp in last:
-            cp.wait_recv()
-        for d in range(3):
-            relay(d, 0).wait_recv()
-            relay(d, 1).wait_recv()
-        for i in range(1, 8):
-            for j in range(i, 8):
-                cols = slice(128 * j, 128 * j + 128)
-                for c in range(2):
-                    for h in range(2):
-                        at = slice(8 * c + 4 * h, 8 * c + 4 * h + 4)
-                        a_s[i, at, :, cols] = a_s[i, at, :, cols] + g[c, h, :, FIRST[i] + j - i]
+    def relay(c, d, h):
+        size = (NX, NY)[h]
+        part = pl.ds(8, 8) if c == 0 else pl.ds(HEAD, REST)
+        got = g.at[core, h, hop(me[h][0], size - 1 - d, size), part]
+        return remote(LATE + 6 * c + 2 * d + h, got, got, sibling)
+
+    def rest_out(d, h):
+        mine = g.at[core, h, me[h][0], pl.ds(HEAD, REST)]
+        if d == 3:
+            return remote(LATE + 18 + h, mine, mine, sibling)
+        return remote(LATE + 12 + 2 * d + h, mine, mine, place[h][0](peers[h][0][d]))
+
+    halves = [(d, h) for d in range(3) for h in range(2)]
+
+    def add_rows(tiles):
+        for i, j in tiles:
+            cols = slice(128 * j, 128 * j + 128)
+            for c in range(2):
+                for h in range(2):
+                    at = slice(8 * c + 4 * h, 8 * c + 4 * h + 4)
+                    a_s[i, at, :, cols] = a_s[i, at, :, cols] + g[c, h, :, FIRST[i] + j - i]
+
+    def add_diagonal(i):
+        for c in range(2):
+            for h in range(2):
+                at = slice(64 * c + 32 * h, 64 * c + 32 * h + 32)
+                ds[at, :] = ds[at, :] + g[c, h, :, FIRST[i]].reshape(32, 128)
 
     def panel(k, _):
         @pl.when(k == 1)
         def _():
-            take_rest()
-            for c in range(2):
-                for h in range(2):
-                    at = slice(64 * c + 32 * h, 64 * c + 32 * h + 32)
-                    ds[at, :] = ds[at, :] + g[c, h, :, FIRST[1]].reshape(32, 128)
+            arrive(row1_own + [relay(0, d, h) for d, h in halves])
+            add_rows([(1, j) for j in range(2, 8)])
+            add_diagonal(1)
+
+        @pl.when(k == 2)
+        def _():
+            arrive([rest_out(3, 0), rest_out(3, 1)] + [relay(1, d, h) for d, h in halves])
+            add_rows([(i, j) for i in range(2, 8) for j in range(i, 8) if j > 2])
+            add_diagonal(2)
 
         prev = jnp.where(k == 0, 8, k - 1)
         dcat = jnp.concatenate([dh_s[prev], dl_s[prev], dh_s[prev]], axis=1)
@@ -394,7 +438,19 @@
 
         @pl.when(k == 0)
         def _():
-            pass_on()
+            for d, h in halves:
+                row1[h][d].wait_recv()
+                relay(0, d, h).start()
+            for h in range(2):
+                arrive(two1[h])
+                for d in range(4):
+                    rest_out(d, h).start()
+
+        @pl.when(k == 1)
+        def _():
+            for d, h in halves:
+                rest_out(d, h).wait_recv()
+                relay(1, d, h).start()
 
         d = split2(ds[...])
         dh_s[k], dl_s[k] = d
@@ -428,11 +484,11 @@
     at_row = row * 8 + lax.broadcasted_iota(jnp.int32, (8, 512), 0)
     at_col = core * 512 + lax.broadcasted_iota(jnp.int32, (8, 512), 1)
     o_ref[0:8, :] = jnp.where(at_col >= at_row, mine, 0.0)
-    for cp in copies:
+    for cp in copies + [relay(c, d, h) for c in range(2) for d, h in halves]:
         cp.wait_send()
-    for d in range(3):
-        relay(d, 0).wait_send()
-        relay(d, 1).wait_send()
+    for d in range(4):
+        for h in range(2):
+            rest_out(d, h).wait_send()
 
 
 def hand_out(all_ref, r_ref, z_ref, x_ref):
@@ -480,15 +536,12 @@
             pltpu.VMEM((1024, 128), BF16),
             tiles(4, 37),
             tiles(4, 36),
-            tiles(4, 37),
-            tiles(4, 36),
-            tiles(4, 10),
-            tiles(4, 9),
-            tiles(4, 10),
-            tiles(4, 9),
-            tiles(8, 4),
-            tiles(8, 4),
-            tiles(8, 3),
+            [[tiles(4, 17), tiles(4, 16)], [tiles(4, 20), tiles(4, 20)]],
+            [[tiles(4, 5), tiles(4, 4)], [tiles(4, 5), tiles(4, 5)]],
+            [[tiles(4, 5), tiles(4, 4)], [tiles(4, 5), tiles(4, 5)]],
+            [tiles(8, 2), tiles(8, 2)],
+            [tiles(8, 2), tiles(8, 2)],
+            [tiles(8, 1), tiles(8, 2)],
             tiles(2, 2, 4, 36),
             pltpu.VMEM((9, 16, 8, 1152), F32),
             pltpu.VMEM((128, 128), F32),

time: 86.7 us -> 85.7 us (0.988)
  Pallas kernels: 85.9 us -> 84.9 us
    pallas_call x1, Pallas kernels: 84.5 us -> 83.5 us  [per_device(): pl.pallas_call(kernel, out_shape=jax.ShapeDtypeStruct((16, 512), F32), in...]
where the time goes in v5:
time: 85.7 us; the launch traced here: 85.5 us
  Pallas kernels  84.9 us (99%)
    pallas_call x1, Pallas kernels, per_device(): pl.pallas_call(kernel, out_shape=jax.ShapeDtypeStruct((16, 512), F32), in...  83.5 us

profile of v5, /device:TPU:1, one launch (start us, length us, event | category | flops | bytes accessed | tf_op | source)
XLA Modules:
  0.0 85.5 jit_solution(12874921516737982908)
XLA Ops:
  0.6 83.5 %shard_map.121.all_ref = f32[16,512]{1,0:T(8,128)} custom-call(f32[384,384]{1,0:T(8,128)} %w_in.1, s32[4,384]{1,0:T(4,128)} %bitcast.9, f32[4,384]{1,0:T(4,128)} %bitcast.10, f32[3,128]{1,0:T(4,128)} %bitcast.11, s32[2,128]{1,0:T(2,128)} %bitcast.12, f32[1,128]{1,0:T(1,128)} %bitcast.13, f32[1,128]{1,0:T(1,128)} %bitcast.14, f32[8,1024]{1,0:T(8,128)} %pr_in.1, ...), custom_call_target="tpu_custom_call" | custom-call | tf_op jit(solution)/shard_map/pallas_call | solution.py:526
  84.2 1.4 %shard_map.122 = (f32[8,512]{1,0:T(8,128)}, f32[1,512]{1,0:T(1,128)}, f32[1,512]{1,0:T(1,128)}) custom-call(f32[16,512]{1,0:T(8,128)} %shard_map.121.all_ref), custom_call_target="tpu_custom_call" | custom-call | tf_op jit(solution)/shard_map/pallas_call | solution.py:567

commit v6 on v5

--- a/solution.py
+++ b/solution.py
@@ -41,17 +41,13 @@
     return jnp.transpose(jnp.broadcast_to(row, (128, 128)))
 
 
-def build_rows(w_ref, st_ref, co_ref, rd_ref, en_ref, cd_ref, br_ref, pr_ref, pi_ref, wcat, hcat, sr, prt, p0, p1):
+def build_rows(w_ref, st_ref, co_ref, en_ref, cd_ref, pr_ref, pi_ref, wcat, hcat, sr, prt, mrow):
     w = split2(w_ref[...])
     wcat[...] = jnp.concatenate([w[0], w[1], w[0]], axis=1)
     cond_row = cd_ref[...]
     cond = spread(cond_row)
     ends = [spread(en_ref[k : k + 1, :].astype(F32)).astype(jnp.int32) for k in range(2)]
     info = spread(jnp.concatenate([pi_ref[...], jnp.zeros((1, 120), F32)], axis=1))[0:8, :]
-    readings = jnp.concatenate([rd_ref[k : k + 1, :] for k in range(3)], axis=1)
-    meas = dot3(split2(jnp.broadcast_to(readings, (8, SENSORS))), w, NT)
-    right = split2(jnp.concatenate([meas, jnp.broadcast_to(cond_row * br_ref[...], (8, BALANCE))], axis=1))
-    rcat = jnp.concatenate([right[0], right[1], right[0]], axis=1)
     for j in range(8):
         cols = slice(128 * j, 128 * j + 128)
         ids = 128 * j + lax.broadcasted_iota(jnp.int32, (128, SENSORS), 0)
@@ -73,24 +69,41 @@
         none = jnp.zeros((80, 128), F32)
         sr[1536:1664, cols] = jnp.concatenate([ph, pm, ph, pl_, ph, pm, none], axis=0).astype(BF16)
         prt[cols, :] = jnp.transpose(jnp.concatenate([ph, ph, pm, ph, pl_, pm, none], axis=0)).astype(BF16)
-        mom = dot(rcat, sr[0:1536, cols])[0:1, :] + jnp.sum(prior * info, axis=0, keepdims=True)
-        for a in range(4):
-            p0[a, HEAD, j : j + 1, :] = mom
-
-
-def build_gram(core, half, en_ref, cd_ref, wcat, hcat, sr, prt, out):
+        mrow[:, cols] = jnp.sum(prior * info, axis=0, keepdims=True)
+
+
+def build_gram(core, half, rd_ref, br_ref, en_ref, cd_ref, wcat, hcat, sr, prt, mrow, out):
     at = [pl.ds(pl.multiple_of(128 * i + 64 * core + 32 * half, 32), 32) for i in range(8)]
-    st = dot(jnp.concatenate([hcat[r, :] for r in at], axis=0), wcat[...], NT)
+    extra = 16 if half == 0 else 0
+    rows = [hcat[r, :] for r in at]
+    if half == 0:
+        readings = jnp.concatenate([rd_ref[k : k + 1, :] for k in range(3)], axis=1)
+        rh, rl = split2(jnp.broadcast_to(readings, (extra, SENSORS)))
+        rows.append(jnp.concatenate([rh, rh, rl], axis=1))
+    st = dot(jnp.concatenate(rows, axis=0), wcat[...], NT)
     ids = lax.broadcasted_iota(jnp.int32, (32, BALANCE), 0) + (64 * core + 32 * half)
     cond = cd_ref[...]
     bal = [
         jnp.where(ids + 128 * i == en_ref[0:1, :], cond, 0.0) - jnp.where(ids + 128 * i == en_ref[1:2, :], cond, 0.0)
         for i in range(8)
     ]
+    prior = [prt[r, :] for r in at]
+    if half == 0:
+        bal.append(jnp.broadcast_to(cond * br_ref[...], (extra, BALANCE)))
+        prior.append(jnp.zeros((extra, 128), BF16))
     th, tl = split2(jnp.concatenate([st, jnp.concatenate(bal, axis=0)], axis=1))
-    lhs = jnp.concatenate([th, tl, th, jnp.concatenate([prt[r, :] for r in at], axis=0)], axis=1)
+    lhs = jnp.concatenate([th, tl, th, jnp.concatenate(prior, axis=0)], axis=1)
+    if half == 0:
+        lhs = jnp.concatenate([lhs[256:, :], lhs[:256, :]], axis=0)
     for j0 in range(0, 8, 2):
-        wide = dot(lhs[0 : 32 * (j0 + 2), :], sr[:, 128 * j0 : 128 * j0 + 256])
+        cols = slice(128 * j0, 128 * j0 + 256)
+        wide = dot(lhs[0 : extra + 32 * (j0 + 2), :], sr[:, cols])
+        if half == 0:
+            mom = wide[0:1, :] + mrow[:, cols]
+            for a in range(4):
+                out[a, HEAD, j0 : j0 + 1, :] = mom[:, 0:128]
+                out[a, HEAD, j0 + 1 : j0 + 2, :] = mom[:, 128:256]
+            wide = wide[extra:, :]
         for j in (j0, j0 + 1):
             for i in range(j + 1):
                 blk = wide[32 * i : 32 * i + 32, 128 * (j - j0) : 128 * (j - j0) + 128]
@@ -106,7 +119,7 @@
     return jnp.broadcast_to(x[row : row + 1, :], (8, 128))
 
 
-NEAR = 8
+NEAR = 7
 
 
 def factor_block(ds, rd, lt, beside):
@@ -187,8 +200,8 @@
 def kernel(
     w_in, st_in, co_in, rd_in, en_in, cd_in, br_in, pr_in, pi_in, t_in, o_ref,
     w_ref, st_ref, co_ref, rd_ref, en_ref, cd_ref, br_ref, pr_ref, pi_ref, t_s,
-    wcat, hcat, sr, prt, p0, p1, r1, q, r2, zs, r3, b4, g,
-    a_s, ds, rd, lt, dh_s, dl_s, rp_s, rt_s, rh_s, rl_s, th_s, tl_s, zv, in_sem, s_sem, r_sem,
+    wcat, hcat, sr, prt, mrow, p0, p1, r1, q, r2, zs, r3, b4, g,
+    a_s, ds, rd, lt, dh_s, dl_s, gh_s, gl_s, rp_s, rt_s, rh_s, rl_s, th_s, tl_s, zv, in_sem, s_sem, r_sem,
 ):
     row = lax.axis_index("rows")
     core = lax.axis_index("cols")
@@ -202,24 +215,22 @@
     for cp in loads:
         cp.start()
 
-    def at_x(v, c=core):
-        return ((v * NY + y) * NZ + z, c)
-
-    def at_y(v, c=core):
-        return ((x * NY + v) * NZ + z, c)
+    def at_x(v):
+        return ((v * NY + y) * NZ + z, core)
+
+    def at_y(v):
+        return ((x * NY + v) * NZ + z, core)
 
     def at_z(v):
         return ((x * NY + y) * NZ + v, core)
 
-    other = 1 - core
-    sibling = (row, other)
+    sibling = (row, 1 - core)
     hop = lambda v, d, n: lax.rem(v + d, n)
     xs = [hop(x, d, NX) for d in range(1, 4)]
     ys = [hop(y, d, NY) for d in range(1, 4)]
     zz = [hop(z, d, NZ) for d in range(1, 8)]
     barrier = pltpu.get_barrier_semaphore()
     friends = [at_x(v) for v in xs] + [at_y(v) for v in ys] + [at_z(v) for v in zz] + [sibling]
-    friends += [at_x(v, other) for v in xs] + [at_y(v, other) for v in ys]
     for to in friends:
         pl.semaphore_signal(barrier, inc=1, device_id=to, device_id_type=MESH)
 
@@ -242,7 +253,7 @@
 
     for cp in loads[:-1]:
         cp.wait()
-    build_rows(w_ref, st_ref, co_ref, rd_ref, en_ref, cd_ref, br_ref, pr_ref, pi_ref, wcat, hcat, sr, prt, p0, p1)
+    build_rows(w_ref, st_ref, co_ref, en_ref, cd_ref, pr_ref, pi_ref, wcat, hcat, sr, prt, mrow)
     me = [(x, y), (y, x)]
     peers = [(xs, ys), (ys, xs)]
     place = [(at_x, at_y), (at_y, at_x)]
@@ -307,10 +318,10 @@
             out.append([send(mine, mine, place[h][1](v)) for v in peers[h][1]])
         return out
 
-    build_gram(core, 0, en_ref, cd_ref, wcat, hcat, sr, prt, p0)
+    build_gram(core, 0, rd_ref, br_ref, en_ref, cd_ref, wcat, hcat, sr, prt, mrow, p0)
     pl.semaphore_wait(barrier, len(friends))
     one0 = [first_out(0, 0)]
-    build_gram(core, 1, en_ref, cd_ref, wcat, hcat, sr, prt, p1)
+    build_gram(core, 1, rd_ref, br_ref, en_ref, cd_ref, wcat, hcat, sr, prt, mrow, p1)
     one0.append(first_out(0, 1))
     one1 = [first_out(1, 0), first_out(1, 1)]
     for i in range(1, 8):
@@ -341,20 +352,25 @@
     two0 = second_back(0)
     arrive(back1)
     two1 = second_back(1)
-    top = []
+    top, own = [], []
     for h in range(2):
         arrive(two0[h])
         mine = g.at[core, h, me[h][0], pl.ds(0, 8)]
-        for c in (core, other):
-            top += [send(mine, mine, place[h][0](v, c)) for v in peers[h][0]]
-        top.append(send(mine, mine, sibling))
+        top.append([send(mine, mine, place[h][0](v)) for v in peers[h][0]])
+        own.append(send(mine, mine, sibling))
     row1, row1_own = [], []
     for h in range(2):
         mine = g.at[core, h, me[h][0], pl.ds(8, 8)]
         row1.append([send(mine, mine, place[h][0](v)) for v in peers[h][0]])
         row1_own.append(send(mine, mine, sibling))
+    for d in range(3):
+        for h in range(2):
+            top[h][d].wait_recv()
+            size = (NX, NY)[h]
+            got = g.at[core, h, hop(me[h][0], size - 1 - d, size), pl.ds(0, 8)]
+            own.append(send(got, got, sibling))
+    arrive(own)
     assert len(copies) == LATE
-    arrive(top)
     for j in range(8):
         for c in range(2):
             for h in range(2):
@@ -422,6 +438,10 @@
 
             return step
 
+        def couple():
+            by = dot(rt_s[k], jnp.concatenate([dh_s[prev], dh_s[prev], dl_s[prev]], axis=0))
+            gh_s[prev], gl_s[prev] = split2(by)
+
         def update(i, j):
             def step():
                 end = min(j + 2, 9)
@@ -433,6 +453,7 @@
             return step
 
         steps = [product(j) for j in range(1, 9, 2)]
+        steps.append(couple)
         steps += [update(i, j) for i in range(1, 8) for j in range(i, 9, 2)]
         factor_block(ds, rd.at[k], lt, [steps[2 * n : 2 * n + 2] for n in range(16)])
 
@@ -466,11 +487,13 @@
     v = [jnp.transpose(a_s[i, :, :, 1024:].reshape(128, 128))[0:8, :] for i in range(7)] + [jnp.transpose(z7)[0:8, :]]
     for i in range(8):
         zv[i : i + 1, :] = v[i][0:1, :]
-    e = [None] * 8
+    e, ek = [None] * 8, None
     for k in range(7, -1, -1):
         e[k] = dot3(split2(v[k]), (dh_s[k], dl_s[k]))
+        if k < 7:
+            e[k] = e[k] - dot3(ek, (gh_s[k], gl_s[k]))
         ek = split2(e[k])
-        for p in range(k - 1, -1, -1):
+        for p in range(k - 2, -1, -1):
             at = slice(128 * k, 128 * k + 128)
             v[p] = v[p] - dot3(ek, (rh_s[p, :, at], rl_s[p, :, at]), NT)
     nxt = dot3(split2(jnp.concatenate(e, axis=1)), (th_s[...], tl_s[...]), NT)
@@ -478,8 +501,8 @@
         o_ref[8:9, 128 * q : 128 * q + 128] = zv[pl.ds(core * 4 + q, 1), :]
     o_ref[9:10, :] = nxt[0:1, :]
     o_ref[10:16, :] = jnp.zeros((6, 512), F32)
-    for k in range(8):
-        a_s[k, :, :, 128 * k : 128 * k + 128] = rd[k].reshape(16, 8, 128)
+    mine = row // 16
+    a_s[mine, :, :, pl.ds(pl.multiple_of(128 * mine, 128), 128)] = rd[mine].reshape(16, 8, 128)
     mine = a_s[row // 16, row % 16, :, pl.ds(pl.multiple_of(core * 512, 512), 512)]
     at_row = row * 8 + lax.broadcasted_iota(jnp.int32, (8, 512), 0)
     at_col = core * 512 + lax.broadcasted_iota(jnp.int32, (8, 512), 1)
@@ -534,6 +557,7 @@
             pltpu.VMEM((1024, 3 * SENSORS), BF16),
             pltpu.VMEM((DEPTH, 1024), BF16),
             pltpu.VMEM((1024, 128), BF16),
+            pltpu.VMEM((1, 1024), F32),
             tiles(4, 37),
             tiles(4, 36),
             [[tiles(4, 17), tiles(4, 16)], [tiles(4, 20), tiles(4, 20)]],
@@ -547,6 +571,8 @@
             pltpu.VMEM((128, 128), F32),
             pltpu.VMEM((8, 128, 128), F32),
             pltpu.VMEM((128, 128), F32),
+            pltpu.VMEM((9, 128, 128), BF16),
+            pltpu.VMEM((9, 128, 128), BF16),
             pltpu.VMEM((9, 128, 128), BF16),
             pltpu.VMEM((9, 128, 128), BF16),
             pltpu.VMEM((384, 1152), BF16),

time: 85.7 us -> 83 us (0.968)
  Pallas kernels: 84.9 us -> 82.2 us
    pallas_call x1, Pallas kernels: 83.5 us -> 80.8 us  [per_device(): pl.pallas_call(kernel, out_shape=jax.ShapeDtypeStruct((16, 512), F32), in...]
where the time goes in v6:
time: 83 us; the launch traced here: 82.8 us
  Pallas kernels  82.2 us (99%)
    pallas_call x1, Pallas kernels, per_device(): pl.pallas_call(kernel, out_shape=jax.ShapeDtypeStruct((16, 512), F32), in...  80.8 us

profile of v6, /device:TPU:1, one launch (start us, length us, event | category | flops | bytes accessed | tf_op | source)
XLA Modules:
  0.0 82.8 jit_solution(4340052728733864498)
XLA Ops:
  0.6 80.8 %shard_map.121.all_ref = f32[16,512]{1,0:T(8,128)} custom-call(f32[384,384]{1,0:T(8,128)} %w_in.1, s32[4,384]{1,0:T(4,128)} %bitcast.9, f32[4,384]{1,0:T(4,128)} %bitcast.10, f32[3,128]{1,0:T(4,128)} %bitcast.11, s32[2,128]{1,0:T(2,128)} %bitcast.12, f32[1,128]{1,0:T(1,128)} %bitcast.13, f32[1,128]{1,0:T(1,128)} %bitcast.14, f32[8,1024]{1,0:T(8,128)} %pr_in.1, ...), custom_call_target="tpu_custom_call" | custom-call | tf_op jit(solution)/shard_map/pallas_call | solution.py:549
  81.4 1.4 %shard_map.122 = (f32[8,512]{1,0:T(8,128)}, f32[1,512]{1,0:T(1,128)}, f32[1,512]{1,0:T(1,128)}) custom-call(f32[16,512]{1,0:T(8,128)} %shard_map.121.all_ref), custom_call_target="tpu_custom_call" | custom-call | tf_op jit(solution)/shard_map/pallas_call | solution.py:593

commit v7 on v6

--- a/solution.py
+++ b/solution.py
@@ -37,6 +37,15 @@
     return dot(a[0], b[0], dims) + (dot(a[0], b[1], dims) + dot(a[1], b[0], dims))
 
 
+def stack2(x):
+    return jnp.concatenate(split2(x), axis=0)
+
+
+def rows_dot(x, hi, lo, dims=NN):
+    both = dot(x, hi, dims) + dot(x, lo, dims)
+    return both[0:8, :] + both[8:16, :]
+
+
 def spread(row):
     return jnp.transpose(jnp.broadcast_to(row, (128, 128)))
 
@@ -48,17 +57,19 @@
     cond = spread(cond_row)
     ends = [spread(en_ref[k : k + 1, :].astype(F32)).astype(jnp.int32) for k in range(2)]
     info = spread(jnp.concatenate([pi_ref[...], jnp.zeros((1, 120), F32)], axis=1))[0:8, :]
-    for j in range(8):
-        cols = slice(128 * j, 128 * j + 128)
-        ids = 128 * j + lax.broadcasted_iota(jnp.int32, (128, SENSORS), 0)
-        h = jnp.zeros((128, SENSORS), F32)
+    twice = lambda v: jnp.concatenate([v, v], axis=1)
+    cond, info, ends = twice(cond), twice(info), [twice(v) for v in ends]
+    for j in range(0, 8, 2):
+        cols = slice(128 * j, 128 * j + 256)
+        ids = 128 * j + lax.broadcasted_iota(jnp.int32, (256, SENSORS), 0)
+        h = jnp.zeros((256, SENSORS), F32)
         for k in range(4):
             h = h + jnp.where(ids == st_ref[k : k + 1, :], co_ref[k : k + 1, :], 0.0)
         hh, hl = split2(h)
         hj = jnp.concatenate([hh, hh, hl], axis=1)
         hcat[cols, :] = hj
         s = dot(wcat[...], hj, NT)
-        bids = 128 * j + lax.broadcasted_iota(jnp.int32, (BALANCE, 128), 1)
+        bids = 128 * j + lax.broadcasted_iota(jnp.int32, (BALANCE, 256), 1)
         bal = jnp.where(bids == ends[0], cond, 0.0) - jnp.where(bids == ends[1], cond, 0.0)
         fh, fl = split2(jnp.concatenate([s, bal], axis=0))
         sr[0:512, cols] = fh
@@ -66,9 +77,12 @@
         sr[1024:1536, cols] = fl
         prior = pr_ref[:, cols]
         ph, pm, pl_ = [part.astype(F32) for part in split3(prior)]
-        none = jnp.zeros((80, 128), F32)
+        none = jnp.zeros((80, 256), F32)
         sr[1536:1664, cols] = jnp.concatenate([ph, pm, ph, pl_, ph, pm, none], axis=0).astype(BF16)
-        prt[cols, :] = jnp.transpose(jnp.concatenate([ph, ph, pm, ph, pl_, pm, none], axis=0)).astype(BF16)
+        packed = jnp.concatenate([ph, ph, pm, ph, pl_, pm, none], axis=0)
+        for n in range(2):
+            half = packed[:, 128 * n : 128 * n + 128]
+            prt[128 * (j + n) : 128 * (j + n) + 128, :] = jnp.transpose(half).astype(BF16)
         mrow[:, cols] = jnp.sum(prior * info, axis=0, keepdims=True)
 
 
@@ -487,16 +501,17 @@
     v = [jnp.transpose(a_s[i, :, :, 1024:].reshape(128, 128))[0:8, :] for i in range(7)] + [jnp.transpose(z7)[0:8, :]]
     for i in range(8):
         zv[i : i + 1, :] = v[i][0:1, :]
-    e, ek = [None] * 8, None
+    nxt = jnp.zeros((8, 512), F32)
+    ek = None
     for k in range(7, -1, -1):
-        e[k] = dot3(split2(v[k]), (dh_s[k], dl_s[k]))
+        e = rows_dot(stack2(v[k]), dh_s[k], dl_s[k])
         if k < 7:
-            e[k] = e[k] - dot3(ek, (gh_s[k], gl_s[k]))
-        ek = split2(e[k])
+            e = e - rows_dot(ek, gh_s[k], gl_s[k])
+        ek = stack2(e)
+        at = slice(128 * k, 128 * k + 128)
         for p in range(k - 2, -1, -1):
-            at = slice(128 * k, 128 * k + 128)
-            v[p] = v[p] - dot3(ek, (rh_s[p, :, at], rl_s[p, :, at]), NT)
-    nxt = dot3(split2(jnp.concatenate(e, axis=1)), (th_s[...], tl_s[...]), NT)
+            v[p] = v[p] - rows_dot(ek, rh_s[p, :, at], rl_s[p, :, at], NT)
+        nxt = nxt + rows_dot(ek, th_s[:, at], tl_s[:, at], NT)
     for q in range(4):
         o_ref[8:9, 128 * q : 128 * q + 128] = zv[pl.ds(core * 4 + q, 1), :]
     o_ref[9:10, :] = nxt[0:1, :]

time: 83 us -> 81.6 us (0.983)
  Pallas kernels: 82.2 us -> 80.7 us
    pallas_call x1, Pallas kernels: 80.8 us -> 79.4 us  [per_device(): pl.pallas_call(kernel, out_shape=jax.ShapeDtypeStruct((16, 512), F32), in...]
where the time goes in v7:
time: 81.6 us; the launch traced here: 81.4 us
  Pallas kernels  80.7 us (99%)
    pallas_call x1, Pallas kernels, per_device(): pl.pallas_call(kernel, out_shape=jax.ShapeDtypeStruct((16, 512), F32), in...  79.4 us

profile of v7, /device:TPU:1, one launch (start us, length us, event | category | flops | bytes accessed | tf_op | source)
XLA Modules:
  0.0 81.4 jit_solution(3898980847422463729)
XLA Ops:
  0.6 79.4 %shard_map.121.all_ref = f32[16,512]{1,0:T(8,128)} custom-call(f32[384,384]{1,0:T(8,128)} %w_in.1, s32[4,384]{1,0:T(4,128)} %bitcast.9, f32[4,384]{1,0:T(4,128)} %bitcast.10, f32[3,128]{1,0:T(4,128)} %bitcast.11, s32[2,128]{1,0:T(2,128)} %bitcast.12, f32[1,128]{1,0:T(1,128)} %bitcast.13, f32[1,128]{1,0:T(1,128)} %bitcast.14, f32[8,1024]{1,0:T(8,128)} %pr_in.1, ...), custom_call_target="tpu_custom_call" | custom-call | tf_op jit(solution)/shard_map/pallas_call | solution.py:564
  80.0 1.4 %shard_map.122 = (f32[8,512]{1,0:T(8,128)}, f32[1,512]{1,0:T(1,128)}, f32[1,512]{1,0:T(1,128)}) custom-call(f32[16,512]{1,0:T(8,128)} %shard_map.121.all_ref), custom_call_target="tpu_custom_call" | custom-call | tf_op jit(solution)/shard_map/pallas_call | solution.py:608

commit v8 on v7

--- a/solution.py
+++ b/solution.py
@@ -418,7 +418,7 @@
                 at = slice(64 * c + 32 * h, 64 * c + 32 * h + 32)
                 ds[at, :] = ds[at, :] + g[c, h, :, FIRST[i]].reshape(32, 128)
 
-    def panel(k, _):
+    def arrivals(k):
         @pl.when(k == 1)
         def _():
             arrive(row1_own + [relay(0, d, h) for d, h in halves])
@@ -431,6 +431,26 @@
             add_rows([(i, j) for i in range(2, 8) for j in range(i, 8) if j > 2])
             add_diagonal(2)
 
+    def relays(k):
+        @pl.when(k == 0)
+        def _():
+            for d, h in halves:
+                row1[h][d].wait_recv()
+                relay(0, d, h).start()
+            for h in range(2):
+                arrive(two1[h])
+                for d in range(4):
+                    rest_out(d, h).start()
+
+        @pl.when(k == 1)
+        def _():
+            for d, h in halves:
+                rest_out(d, h).wait_recv()
+                relay(1, d, h).start()
+
+    def panel(k, low):
+        if low == 1:
+            arrivals(k)
         prev = jnp.where(k == 0, 8, k - 1)
         dcat = jnp.concatenate([dh_s[prev], dl_s[prev], dh_s[prev]], axis=1)
 
@@ -466,36 +486,27 @@
 
             return step
 
-        steps = [product(j) for j in range(1, 9, 2)]
+        steps = [product(j) for j in range(low - 1 + low % 2, 9, 2)]
         steps.append(couple)
-        steps += [update(i, j) for i in range(1, 8) for j in range(i, 9, 2)]
+        steps += [update(i, j) for i in range(low, 8) for j in range(i, 9, 2)]
         factor_block(ds, rd.at[k], lt, [steps[2 * n : 2 * n + 2] for n in range(16)])
 
-        @pl.when(k == 0)
-        def _():
-            for d, h in halves:
-                row1[h][d].wait_recv()
-                relay(0, d, h).start()
-            for h in range(2):
-                arrive(two1[h])
-                for d in range(4):
-                    rest_out(d, h).start()
-
-        @pl.when(k == 1)
-        def _():
-            for d, h in halves:
-                rest_out(d, h).wait_recv()
-                relay(1, d, h).start()
-
+        if low == 1:
+            relays(k)
         d = split2(ds[...])
         dh_s[k], dl_s[k] = d
         nxt = pl.ds(pl.multiple_of(128 * k + 128, 128), 128)
         c = dot3(d, split2(a_s[k, :, :, nxt].reshape(128, 128)))
         ds[...] = a_s[k + 1, :, :, nxt].reshape(128, 128) - dot3(split2(jnp.transpose(c)), split2(c))
-        return 0
 
     ds[...] = a_s[0, :, :, 0:128].reshape(128, 128)
-    lax.fori_loop(0, 8, panel, 0)
+    for begin, end, low in ((0, 4, 1), (4, 8, 4)):
+
+        def one(k, done, low=low):
+            panel(k, low)
+            return done
+
+        lax.fori_loop(begin, end, one, 0)
 
     z7 = dot3((dh_s[7], dl_s[7]), split2(a_s[7, :, :, 1024:].reshape(128, 128)))
     v = [jnp.transpose(a_s[i, :, :, 1024:].reshape(128, 128))[0:8, :] for i in range(7)] + [jnp.transpose(z7)[0:8, :]]

time: 81.6 us -> 80.9 us (level)
  no operation moved by 1% of the time
where the time goes in v8:
time: 80.9 us; the launch traced here: 80.7 us
  Pallas kernels  80.1 us (99%)
    pallas_call x1, Pallas kernels, per_device(): pl.pallas_call(kernel, out_shape=jax.ShapeDtypeStruct((16, 512), F32), in...  78.7 us

profile of v8, /device:TPU:1, one launch (start us, length us, event | category | flops | bytes accessed | tf_op | source)
XLA Modules:
  0.0 80.7 jit_solution(4128297653128511185)
XLA Ops:
  0.6 78.7 %shard_map.121.all_ref = f32[16,512]{1,0:T(8,128)} custom-call(f32[384,384]{1,0:T(8,128)} %w_in.1, s32[4,384]{1,0:T(4,128)} %bitcast.9, f32[4,384]{1,0:T(4,128)} %bitcast.10, f32[3,128]{1,0:T(4,128)} %bitcast.11, s32[2,128]{1,0:T(2,128)} %bitcast.12, f32[1,128]{1,0:T(1,128)} %bitcast.13, f32[1,128]{1,0:T(1,128)} %bitcast.14, f32[8,1024]{1,0:T(8,128)} %pr_in.1, ...), custom_call_target="tpu_custom_call" | custom-call | tf_op jit(solution)/shard_map/pallas_call | solution.py:575
  79.4 1.4 %shard_map.122 = (f32[8,512]{1,0:T(8,128)}, f32[1,512]{1,0:T(1,128)}, f32[1,512]{1,0:T(1,128)}) custom-call(f32[16,512]{1,0:T(8,128)} %shard_map.121.all_ref), custom_call_target="tpu_custom_call" | custom-call | tf_op jit(solution)/shard_map/pallas_call | solution.py:619
